TPU v7x, 512 devices: a whole 4x8x8 slice. The times are simulated.
512 devices in a mesh: dp: 32 (over x, y), tensor: 16 (over z, core).
Axes of the slice: x: 4, y: 8, z: 8, core: 2. Of those that a mesh axis runs over, the one named last changes fastest.
Arguments:
- activations: bfloat16 [32, 1024, 2048], P('dp', 'tensor'), may hold values from -6 to 6
- out_grad: bfloat16 [32, 1024, 7168], P('dp', None, 'tensor'), may hold values from -0.1875 to 0.1875
- feedback: bfloat16 [32, 2048, 7168], P('dp', None, 'tensor'), may hold values from -3 to 3
- q_prev: float32 [7168, 64], P('tensor'), may hold values from -6 to 6
Outputs:
- new_feedback: bfloat16 [32, 2048, 7168], P('dp', None, 'tensor')
- p_orth: float32 [2048, 64], P('tensor')
- q_new: float32 [7168, 64], P('tensor')
All inputs are finite; a program needn't handle non-finite values.
Results may differ from a plain program's by a relative error of at most 0.00045.
Values may be sent and summed in bfloat16 or wider, within the bound.
No kernel may reach another device: no remote copies, remote signals or barrier semaphores. Data moves between devices by JAX's collectives and lax.ppermute only.
A program may use at most 64 MiB of HBM per device.

v0:
```python
import jax
import jax.numpy as jnp
from jax import lax
from jax.sharding import PartitionSpec as P


def orthonormal(matrix):
    columns = matrix.shape[1]
    order = jnp.arange(columns)

    def sweep(position, current):
        column = current[:, position]
        column = column / jnp.sqrt(jnp.sum(column * column) + 1e-06)
        projected = jnp.dot(column, current, precision=lax.Precision.HIGHEST)
        later = jnp.where(order > position, projected, jnp.zeros_like(projected))
        current = current - column[:, None] * later[None, :]
        return jnp.where((order == position)[None, :], column[:, None], current)

    return lax.fori_loop(0, columns, sweep, matrix)


def body(activations, out_grad, feedback, q_prev):
    cotangent = out_grad[0]
    width = activations.shape[2]
    replicas = lax.axis_size("dp")
    row_share = width // lax.axis_size("tensor")
    gradient = lax.dot_general(
        lax.all_gather(activations, "tensor", axis=1, tiled=True)[0],
        cotangent,
        (((0,), (0,)), ((), ())),
        preferred_element_type=jnp.float32,
    )
    corrected = gradient + feedback[0].astype(jnp.float32)
    p_terms = jnp.dot(corrected, q_prev, precision=lax.Precision.HIGHEST)
    p_sum = lax.psum(p_terms, ("dp", "tensor")) / replicas
    p_full = orthonormal(p_sum)
    first_row = lax.axis_index("tensor") * row_share
    p_mine = lax.dynamic_slice_in_dim(p_full, first_row, row_share, 0)
    q_terms = lax.dot_general(
        corrected, p_full, (((0,), (0,)), ((), ())), precision=lax.Precision.HIGHEST
    )
    q_new = lax.psum(q_terms, "dp") / replicas
    decompressed = jnp.dot(p_full, q_new.T, precision=lax.Precision.HIGHEST)
    new_feedback = (corrected - decompressed).astype(jnp.bfloat16)[None]
    return (new_feedback, p_mine, q_new)


def solution(mesh):
    in_specs = (
        P("dp", "tensor", None),
        P("dp", None, "tensor"),
        P("dp", None, "tensor"),
        P("tensor", None),
    )
    out_specs = (P("dp", None, "tensor"), P("tensor", None), P("tensor", None))
    return jax.shard_map(body, mesh=mesh, in_specs=in_specs, out_specs=out_specs, check_vma=False)
```

profile of v0, /device:TPU:12, one launch (start us, length us, event | category | flops | bytes accessed | tf_op | source)
XLA Modules:
  0.0 637.8 jit_solution(15784140948567281778)
XLA Ops:
  7.2 0.7 all-gather.2.cloned.1.call-update
  8.0 52.4 %all-gather.2.cloned.1.call-done = bf16[1,1024,2048]{2,1,0:T(8,128)(2,1)} async-done(((bf16[1,64,2048]{2,1,0:T(8,128)(2,1)}), bf16[1,1024,2048]{2,1,0:T(8,128)(2,1)}) %all-gather.2.cloned.1.call-update) | async-done | bytes 4194320 | tf_op jit(solution)/shard_map/all_gather | solution.py:28
  60.4 4.8 convert_add_fusion
  65.2 1.8 copy-done.1
  67.0 3.3 fusion.9
  70.4 266.7 %all-reduce.3.cloned.1.call-done = f32[2048,64]{0,1:T(8,128)} async-done(((f32[2048,64]{0,1:T(8,128)}), f32[2048,64]{0,1:T(8,128)}) %all-reduce.3.cloned.1.call-update) | async-done | bytes 524304 | tf_op jit(solution)/shard_map/psum | solution.py:35
  337.0 1.1 broadcast_multiply_fusion
  338.1 131.2 %while.15 = (s32[]{:T(128)}, f32[2048,64]{0,1:T(8,128)S(1)}, s32[]{:T(128)}, f32[]{:T(128)}) while((s32[]{:T(128)}, f32[2048,64]{0,1:T(8,128)S(1)}, s32[]{:T(128)}, f32[]{:T(128)}) %tuple.39), condition=%wide.region_3.4_spmd.clone.clone, body=%wide.region_1.3_spmd.clone.clone.sunk | while | flops 1972418 | bytes 1614561 | solution.py:19
  338.1 0.6 multiply_reduce_fusion.2
  340.2 0.6 multiply_reduce_fusion.2
  344.3 0.6 multiply_reduce_fusion.2
  346.3 0.6 multiply_reduce_fusion.2
  350.4 0.6 multiply_reduce_fusion.2
  352.5 0.6 multiply_reduce_fusion.2
  356.6 0.6 multiply_reduce_fusion.2
  358.6 0.6 multiply_reduce_fusion.2
  362.7 0.6 multiply_reduce_fusion.2
  364.8 0.6 multiply_reduce_fusion.2
  370.9 0.6 multiply_reduce_fusion.2
  377.1 0.6 multiply_reduce_fusion.2
  379.2 0.6 multiply_reduce_fusion.2
  383.3 0.6 multiply_reduce_fusion.2
  385.3 0.6 multiply_reduce_fusion.2
  389.4 0.6 multiply_reduce_fusion.2
  391.5 0.6 multiply_reduce_fusion.2
  395.6 0.6 multiply_reduce_fusion.2
  397.6 0.6 multiply_reduce_fusion.2
  401.7 0.6 multiply_reduce_fusion.2
  403.8 0.6 multiply_reduce_fusion.2
  409.9 0.6 multiply_reduce_fusion.2
  416.1 0.6 multiply_reduce_fusion.2
  418.1 0.6 multiply_reduce_fusion.2
  422.2 0.6 multiply_reduce_fusion.2
  424.3 0.6 multiply_reduce_fusion.2
  428.4 0.6 multiply_reduce_fusion.2
  430.4 0.6 multiply_reduce_fusion.2
  434.5 0.6 multiply_reduce_fusion.2
  436.6 0.6 multiply_reduce_fusion.2
  440.7 0.6 multiply_reduce_fusion.2
  442.7 0.6 multiply_reduce_fusion.2
  448.9 0.6 multiply_reduce_fusion.2
  455.0 0.6 multiply_reduce_fusion.2
  457.1 0.6 multiply_reduce_fusion.2
  469.4 6.1 fusion.10
  475.5 0.6 constant_dynamic-slice_fusion
  476.2 148.4 %all-reduce.5.cloned.1.call-done = f32[448,64]{0,1:T(8,128)} async-done(((f32[448,64]{0,1:T(8,128)}), f32[448,64]{0,1:T(8,128)}) %all-reduce.5.cloned.1.call-update) | async-done | bytes 114704 | tf_op jit(solution)/shard_map/psum | solution.py:42
  624.5 0.9 broadcast_multiply_fusion.1
  625.5 5.8 fusion.7
  (297 shorter events, 62.5 us)
Async XLA Ops:
  7.2 53.2 %copy-start = (bf16[1,1024,448]{1,2,0:T(8,128)(2,1)S(1)}, bf16[1,1024,448]{1,2,0:T(8,128)(2,1)}, u32[]{:S(2)}) copy-start(bf16[1,1024,448]{1,2,0:T(8,128)(2,1)} %param.7) | copy-start | bytes 2752516
  7.2 53.2 %all-gather.2.cloned.1.call-start = ((), (), s32[]{:S(2)}) async-start(), calls=%async_computation | async-start | bytes 4456448 | tf_op jit(solution)/shard_map/all_gather | solution.py:28
  7.9 59.1 %copy-start.3 = (f32[448,64]{0,1:T(8,128)S(1)}, f32[448,64]{0,1:T(8,128)}, u32[]{:S(2)}) copy-start(f32[448,64]{0,1:T(8,128)} %param.9) | copy-start | bytes 344068
  7.9 329.1 %all-reduce.3.cloned.1.call-start = ((), (), s32[]{:S(2)}) async-start(), calls=%async_computation.1 | async-start | bytes 1048576 | tf_op jit(solution)/shard_map/psum | solution.py:35
  65.2 1.8 copy-start.1
  70.3 554.2 %all-reduce.5.cloned.1.call-start = ((), (), s32[]{:S(2)}) async-start(), calls=%async_computation.2 | async-start | bytes 262144 | tf_op jit(solution)/shard_map/psum | solution.py:42
  625.4 5.8 copy-start.2
Sparse Core Ops, SparseCore 0:
  10.1 50.1 all-gather.1
  70.4 266.5 all-reduce.2
  475.7 148.8 all-reduce.4
where the time goes:
time: 639 us; the launch traced here: 638 us
  waiting for transfers between devices  468 us (73%)
  other arithmetic  53.4 us (8%)
  matrix products  52.7 us (8%)
  loops' own time  47.1 us (7%)
  between operations  13.8 us (2%)
    psum x1, waiting for transfers between devices, body(): p_sum = lax.psum(p_terms, ('dp', 'tensor')) / replicas  267 us
    psum x1, waiting for transfers between devices, body(): q_new = lax.psum(q_terms, 'dp') / replicas  148 us
    all_gather x1, waiting for transfers between devices, body(): lax.all_gather(activations, 'tensor', axis=1, tiled=True)[0]  52.4 us
    another operation x1, loops' own time, orthonormal(): return lax.fori_loop(0, columns, sweep, matrix)  47.1 us
    reduce_sum x64, other arithmetic, sweep(): column = column / jnp.sqrt(jnp.sum(column * column) + 1e-06)  39.8 us
    dot_general x64, matrix products, sweep(): projected = jnp.dot(column, current, precision=lax.Precision.HIGHEST)  32.7 us
  transfers between devices with their start and end apart: 3, of which 3 were waited for; matrix products, arithmetic and copies ran while one was open for 0% of the time, Pallas kernels for 0%

commit v1 on v0

v1 whole, which is shorter than its diff:
```python
import jax
import jax.numpy as jnp
from jax import lax
from jax.experimental import pallas as pl
from jax.experimental.pallas import tpu as pltpu
from jax.sharding import Mesh
from jax.sharding import PartitionSpec as P

LANES = 128
SUBLANES = 8
EPS = 1e-06
BF16 = jnp.bfloat16
F32 = jnp.float32


def split3(value):
    high = value.astype(BF16)
    rest = value - high.astype(F32)
    middle = rest.astype(BF16)
    low = (rest - middle.astype(F32)).astype(BF16)
    return high, middle, low


def stacked(value):
    return jnp.concatenate(split3(value), axis=0)


def unstacked(value):
    rows = value.shape[0] // 3
    return (value[2 * rows :] + value[rows : 2 * rows]) + value[:rows]


def exact_dot(value, exact):
    return unstacked(jnp.dot(stacked(value), exact, preferred_element_type=F32))


def exact_dot_t(value, exact):
    return unstacked(
        lax.dot_general(
            stacked(value), exact, (((1,), (1,)), ((), ())), preferred_element_type=F32
        )
    )


def call(kernel, out_shape, *args, grid=None, vmem=32, **kw):
    shapes = jax.tree.map(lambda s: jax.ShapeDtypeStruct(*s), out_shape, is_leaf=lambda s: isinstance(s, tuple) and isinstance(s[0], tuple))
    return pl.pallas_call(
        kernel,
        out_shape=shapes,
        compiler_params=pltpu.CompilerParams(vmem_limit_bytes=vmem * 2**20),
        **({} if grid is None else {"grid": grid}),
        **kw,
    )(*args)


def cotangent_kernel(q_ref, g_ref, out_ref):
    rank = q_ref.shape[0]
    half = rank // 2
    product = exact_dot(q_ref[...], g_ref[...])
    low = lax.broadcasted_iota(jnp.int32, (half, LANES), 1) < LANES // 2
    for tile in range(product.shape[1] // LANES):
        block = product[:, tile * LANES : (tile + 1) * LANES]
        top, bottom = block[:half], block[half:]
        out_ref[2 * tile] = jnp.where(low, top, pltpu.roll(bottom, LANES // 2, 1))
        out_ref[2 * tile + 1] = jnp.where(low, pltpu.roll(top, LANES // 2, 1), bottom)


def feedback_kernel(q_ref, f_ref, out_ref):
    product = exact_dot(q_ref[...], f_ref[...])
    for tile in range(out_ref.shape[0]):
        out_ref[tile] = product[:, tile * LANES : (tile + 1) * LANES]


def left_kernel(y_ref, a_ref, pf_ref, out_ref):
    total = y_ref[0]
    for source in range(1, y_ref.shape[0]):
        total = total + y_ref[source]
    tokens = a_ref.shape[0]
    mine = jnp.concatenate([total[:, :tokens], total[:, tokens:]], axis=0)
    product = exact_dot(mine, a_ref[...])
    for tile in range(out_ref.shape[0]):
        out_ref[tile] = product[:, tile * LANES : (tile + 1) * LANES] + pf_ref[tile]


def pair_kernel(x_ref, out_ref):
    out_ref[...] = x_ref[0] + x_ref[1]


def share_kernel(fold, scale, x_ref, out_ref):
    total = x_ref[0]
    for source in range(1, x_ref.shape[0]):
        total = total + x_ref[source]
    step = fold
    while step < SUBLANES:
        total = total + pltpu.roll(total, step, 0)
        step *= 2
    total = total * scale
    for target in range(out_ref.shape[0]):
        out_ref[target] = total


def orthonormal_kernel(core_ref, mine_ref, other_ref, x_ref):
    tiles, rank, _ = x_ref.shape
    part = tiles // 2
    core = core_ref[0]
    x_ref[pl.ds(core * part, part)] = mine_ref[...]
    x_ref[pl.ds((1 - core) * part, part)] = other_ref[...]
    for first in range(0, rank, SUBLANES):

        def sweep(step, carry, first=first):
            position = first + step
            rows = [x_ref[tile, pl.ds(position, 1), :] for tile in range(tiles)]
            dots = x_ref[0, first:, :] * rows[0]
            square = rows[0] * rows[0]
            for tile in range(1, tiles):
                dots = dots + x_ref[tile, first:, :] * rows[tile]
                square = square + rows[tile] * rows[tile]
            dots = jnp.sum(dots, axis=1, keepdims=True)
            square = jnp.sum(square, axis=1, keepdims=True) + EPS
            order = lax.broadcasted_iota(jnp.int32, dots.shape, 0) + first
            factor = jnp.where(order > position, dots / square, 0.0)
            scale = jnp.where(order == position, 1.0 / jnp.sqrt(square), 1.0)
            for tile in range(tiles):
                x_ref[tile, first:, :] = x_ref[tile, first:, :] * scale - rows[tile] * factor
            return carry

        lax.fori_loop(0, SUBLANES, sweep, 0)


def wide(p_ref):
    return jnp.concatenate([p_ref[tile] for tile in range(p_ref.shape[0])], axis=1)


def right_kernel(p_ref, a_ref, f_ref, g_ref, out_ref):
    p = wide(p_ref)
    tokens = exact_dot_t(p, a_ref[...])
    product = exact_dot_t(p, f_ref[...]) + exact_dot_t(tokens, g_ref[...])
    width = product.shape[1]
    for tile in range(out_ref.shape[0]):
        block = product[:, tile * LANES : min(width, (tile + 1) * LANES)]
        if block.shape[1] < LANES:
            block = jnp.concatenate([block, jnp.zeros((block.shape[0], LANES - block.shape[1]), F32)], axis=1)
        out_ref[tile] = block


def feedback_out_kernel(q_ref, p_ref, g_ref, a_ref, f_ref, fb_ref, qt_ref):
    width = qt_ref.shape[1]
    q_wide = wide(q_ref)[:, :width]
    qt_ref[...] = q_wide
    q1, q2, q3 = split3(q_wide.T)
    p1, p2, p3 = split3(wide(p_ref))
    left = jnp.concatenate([q3, q1, q2, q2, q1, q1], axis=1)
    right = jnp.concatenate([p1, p3, p2, p1, p2, p1], axis=0)
    low_rank = jnp.dot(left, right, preferred_element_type=F32)
    gradient = jnp.dot(g_ref[...], a_ref[...], preferred_element_type=F32)
    corrected = gradient + f_ref[...].astype(F32)
    fb_ref[...] = (corrected - low_rank).astype(BF16)


def body(activations, out_grad, feedback, q_prev):
    xy, xyz, tensor = ("x", "y"), ("x", "y", "z"), ("z", "c")
    a = activations[0]
    gt = out_grad[0].T
    ft = feedback[0].T
    qt = q_prev.T
    width, columns = ft.shape[1], ft.shape[0]
    rank, tokens = qt.shape[0], gt.shape[1]
    replicas = lax.axis_size(xy)
    chips = lax.axis_size(xyz)
    members = lax.axis_size(tensor)
    core = lax.axis_index("c")
    tiles = width // LANES

    a_full = lax.all_gather(a, tensor, axis=0, tiled=True)
    y = call(cotangent_kernel, ((members, rank // 2, LANES), F32), qt, gt)
    y = lax.all_to_all(y, tensor, 0, 0)
    p_feedback = call(feedback_kernel, ((tiles, rank, LANES), F32), qt, ft)
    p = call(left_kernel, ((tiles, rank, LANES), F32), y, a, p_feedback)
    p = lax.all_to_all(p.reshape(2, tiles // 2 * rank, LANES), "c", 0, 0)
    p = call(pair_kernel, ((tiles // 2 * rank, LANES), F32), p)
    rows = tiles // 2 * rank // chips
    groups = tiles // 2 * rank // SUBLANES
    p = lax.all_to_all(p.reshape(chips, rows, LANES), xyz, 0, 0)
    p = call(
        lambda *refs: share_kernel(rows, 1.0 / replicas, *refs),
        ((groups, SUBLANES, LANES), F32),
        p.reshape(groups, SUBLANES, LANES),
    )
    p = lax.all_to_all(p.reshape(chips, rows, LANES), xyz, 0, 0)
    p = p.reshape(tiles // 2, rank, LANES)
    other = lax.ppermute(p, "c", [(0, 1), (1, 0)])
    vmem = pl.BlockSpec(memory_space=pltpu.VMEM)
    p_orth = call(
        orthonormal_kernel,
        ((tiles, rank, LANES), F32),
        core.astype(jnp.int32)[None],
        p,
        other,
        in_specs=[pl.BlockSpec(memory_space=pltpu.SMEM), vmem, vmem],
        out_specs=vmem,
    )
    p_mine = lax.dynamic_index_in_dim(p_orth, lax.axis_index(tensor), 0, keepdims=False).T

    q_tiles = -(-columns // LANES)
    q = call(right_kernel, ((q_tiles, rank, LANES), F32), p_orth, a_full, ft, gt)
    q_rows = q_tiles * rank // replicas
    q_groups = q_tiles * rank // SUBLANES
    q = lax.all_to_all(q.reshape(replicas, q_rows, LANES), xy, 0, 0)
    q = call(
        lambda *refs: share_kernel(q_rows, 1.0 / replicas, *refs),
        ((q_groups, SUBLANES, LANES), F32),
        q.reshape(q_groups, SUBLANES, LANES),
    )
    q = lax.all_to_all(q.reshape(replicas, q_rows, LANES), xy, 0, 0)
    q = q.reshape(q_tiles, rank, LANES)

    block = 2 * LANES
    fbt, q_new = call(
        feedback_out_kernel,
        [((columns, width), BF16), ((rank, columns), F32)],
        q,
        p_orth,
        gt,
        a_full,
        ft,
        grid=(width // block,),
        in_specs=[
            pl.BlockSpec((q_tiles, rank, LANES), lambda i: (0, 0, 0)),
            pl.BlockSpec((block // LANES, rank, LANES), lambda i: (i, 0, 0)),
            pl.BlockSpec((columns, tokens), lambda i: (0, 0)),
            pl.BlockSpec((tokens, block), lambda i: (0, i)),
            pl.BlockSpec((columns, block), lambda i: (0, i)),
        ],
        out_specs=[
            pl.BlockSpec((columns, block), lambda i: (0, i)),
            pl.BlockSpec((rank, columns), lambda i: (0, 0)),
        ],
    )
    return fbt.T[None], p_mine, q_new.T


def solution(mesh):
    sizes = (4, 8, 8, 2)
    fine = Mesh(mesh.devices.reshape(sizes), ("x", "y", "z", "c"))
    dp, tensor = ("x", "y"), ("z", "c")
    in_specs = (
        P(dp, tensor, None),
        P(dp, None, tensor),
        P(dp, None, tensor),
        P(tensor, None),
    )
    out_specs = (P(dp, None, tensor), P(tensor, None), P(tensor, None))
    return jax.shard_map(body, mesh=fine, in_specs=in_specs, out_specs=out_specs, check_vma=False)
```

time: 639 us -> 159 us (0.25)
  the two profiles are of different devices: /device:TPU:12 before, /device:TPU:8 now
where the time goes in v1:
time: 159 us; the launch traced here: 158 us
  blocking collectives  73.3 us (46%)
  Pallas kernels  22.9 us (14%)
  waiting for transfers between devices  22 us (14%)
  starting transfers between devices  16.9 us (11%)
  between operations  14.2 us (9%)
  local copies, waits for them, and re-layouts  8.74 us (5%)
    all_to_all x2, blocking collectives, body(): p = lax.all_to_all(p.reshape(chips, rows, LANES), xyz, 0, 0)  54.6 us
    pallas_call x9, Pallas kernels, call(): pl.pallas_call(kernel, out_shape=shapes, compiler_params=pltpu.CompilerPa...  22.9 us
    all_to_all x1, blocking collectives, body(): q = lax.all_to_all(q.reshape(replicas, q_rows, LANES), xy, 0, 0)  14.1 us
    all_to_all x1, waiting for transfers between devices, body(): y = lax.all_to_all(y, tensor, 0, 0)  10.6 us
    all_to_all x1, starting transfers between devices, body(): y = lax.all_to_all(y, tensor, 0, 0)  10.6 us
    all_to_all x1, waiting for transfers between devices, body(): q = lax.all_to_all(q.reshape(replicas, q_rows, LANES), xy, 0, 0)  9.24 us
    unnamed x20, local copies, waits for them, and re-layouts  8.11 us
    all_to_all x1, blocking collectives, body(): p = lax.all_to_all(p.reshape(2, tiles // 2 * rank, LANES), 'c', 0, 0)  4.59 us
  transfers between devices with their start and end apart: 4, of which 3 were waited for; matrix products, arithmetic and copies ran while one was open for 0% of the time, Pallas kernels for 8%

profile of v1, /device:TPU:8, one launch (start us, length us, event | category | flops | bytes accessed | tf_op | source)
XLA Modules:
  0.0 158.0 jit_solution(7518527910623220089)
XLA Ops:
  7.2 0.0 copy-start.2
  7.2 0.0 all-gather.3.cloned.1.call-start
  7.2 0.7 all-gather.3.cloned.1.call-update
  7.9 0.0 copy-start.3
  7.9 1.2 copy-done.3
  9.1 0.0 copy-start.6
  9.1 0.9 copy-done.6
  10.0 0.0 copy-start.7
  10.0 1.2 shard_map.67
  11.2 0.0 copy-start.5
  11.2 10.6 %all-to-all-start = ((f32[16,32,128]{2,1,0:T(8,128)}), f32[16,32,128]{2,1,0:T(8,128)S(1)}, u32[]{:S(2)}, u32[]{:S(2)}) async-start(f32[16,32,128]{2,1,0:T(8,128)} %shard_map.67), calls=%async_computation | async-start | bytes 524288 | tf_op jit(solution)/shard_map/all_to_all | solution.py:176
  21.7 0.0 copy-done.2
  21.7 0.0 copy-done.7
  21.7 0.6 shard_map.68.pf_ref
  22.3 10.6 %all-to-all-done.y_ref = f32[16,32,128]{2,1,0:T(8,128)S(1)} async-done(((f32[16,32,128]{2,1,0:T(8,128)}), f32[16,32,128]{2,1,0:T(8,128)S(1)}, u32[]{:S(2)}, u32[]{:S(2)}) %all-to-all-start) | async-done | bytes 262176 | tf_op jit(solution)/shard_map/all_to_all | solution.py:176
  32.9 0.0 copy-done.5
  32.9 0.4 shard_map.69
  33.3 4.6 %all_to_all.30.x_ref = f32[2,512,128]{2,1,0:T(8,128)S(1)} all-to-all(f32[2,512,128]{2,1,0:T(8,128)S(1)} %bitcast.33), channel_id=1, replica_groups=mesh['x'=4,'y'=8,'z'=8,'c'=2] {'c'}, dimensions={0} | all-to-all | bytes 1048576 | tf_op jit(solution)/shard_map/all_to_all | solution.py:179
  37.9 0.0 copy-start.4
  38.0 30.8 %all_to_all.31 = f32[256,2,128]{2,1,0:T(2,128)S(1)} all-to-all(f32[256,2,128]{2,1,0:T(2,128)S(1)} %bitcast.34), channel_id=1, replica_groups=mesh['x'=4,'y'=8,'z'=8,'c'=2] {'x','y','z'}, dimensions={0} | all-to-all | bytes 524288 | tf_op jit(solution)/shard_map/all_to_all | solution.py:183
  68.8 0.1 shard_map.71
  68.9 23.8 %all_to_all.32 = f32[256,2,128]{2,1,0:T(2,128)S(1)} all-to-all(f32[256,2,128]{2,1,0:T(2,128)S(1)} %bitcast.36), channel_id=1, replica_groups=mesh['x'=4,'y'=8,'z'=8,'c'=2] {'x','y','z'}, dimensions={0} | all-to-all | bytes 524288 | tf_op jit(solution)/shard_map/all_to_all | solution.py:189
  92.7 1.9 %collective-permute-start = (f32[8,64,128]{2,1,0:T(8,128)S(1)}, f32[8,64,128]{2,1,0:T(8,128)S(1)}, u32[]{:S(2)}, u32[]{:S(2)}) collective-permute-start(f32[8,64,128]{2,1,0:T(8,128)S(1)} %bitcast.38), channel_id=1, source_target_pairs={{0,1},{1,0},{2,3},{3,2},{4,5},{5,4},{6,7},{7,6},{8,9},{9,8},{10,11... | collective-permute-start | bytes 786440 | tf_op jit(solution)/shard_map/ppermute | solution.py:191
  94.6 1.5 collective-permute-done.other_ref
  96.1 0.0 copy-start.8
  96.1 0.7 copy-done.8
  96.8 0.0 copy-start.9
  96.8 0.9 copy-done.9
  97.8 10.0 %shard_map.72.p_ref = f32[16,64,128]{2,1,0:T(8,128)S(1)} custom-call(s32[1]{0:T(128)} %bitcast.core_ref, f32[8,64,128]{2,1,0:T(8,128)S(1)} %bitcast.39, f32[8,64,128]{2,1,0:T(8,128)S(1)} %copy-done.9), custom_call_target="tpu_custom_call" | custom-call | tf_op jit(solution)/shard_map/pallas_call | solution.py:47
  107.8 0.0 all-gather.3.cloned.1.call-done
  107.8 0.0 copy-done.4
  107.8 0.0 copy-start
  107.8 2.2 %copy-done = bf16[1,1024,2048]{2,1,0:T(8,128)(2,1)S(1)} copy-done((bf16[1,1024,2048]{2,1,0:T(8,128)(2,1)S(1)}, bf16[1,1024,2048]{2,1,0:T(8,128)(2,1)}, u32[]{:S(2)}) %copy-start) | copy-done | bytes 4194328
  110.0 2.3 %shard_map.73 = f32[4,64,128]{2,1,0:T(8,128)S(1)} custom-call(f32[16,64,128]{2,1,0:T(8,128)S(1)} %shard_map.72.p_ref, bf16[1024,2048]{1,0:T(8,128)(2,1)S(1)} %bitcast.25, bf16[448,2048]{1,0:T(8,128)(2,1)S(1)} %bitcast.28, bf16[448,1024]{1,0:T(8,128)(2,1)S(1)} %bitcast.31), custom_call_target="tpu_custom_call" | custom-call | tf_op jit(solution)/shard_map/pallas_call | solution.py:47
  112.3 14.1 %all_to_all.33.refs_0_ = f32[32,8,128]{2,1,0:T(8,128)S(1)} all-to-all(f32[32,8,128]{2,1,0:T(8,128)S(1)} %bitcast.43), channel_id=1, replica_groups=mesh['x'=4,'y'=8,'z'=8,'c'=2] {'x','y'}, dimensions={0} | all-to-all | bytes 262144 | tf_op jit(solution)/shard_map/all_to_all | solution.py:208
  126.4 0.7 shard_map.74
  127.1 4.3 %all-to-all-start.5 = ((f32[32,8,128]{2,1,0:T(8,128)}), f32[32,8,128]{2,1,0:T(8,128)S(1)}, u32[]{:S(2)}, u32[]{:S(2)}) async-start(f32[32,8,128]{2,1,0:T(8,128)} %shard_map.74), calls=%async_computation.5 | async-start | bytes 262144 | tf_op jit(solution)/shard_map/all_to_all | solution.py:214
  131.5 0.6 dynamic-slice_bitcast_fusion
  132.1 9.2 %all-to-all-done.5 = f32[32,8,128]{2,1,0:T(8,128)S(1)} async-done(((f32[32,8,128]{2,1,0:T(8,128)}), f32[32,8,128]{2,1,0:T(8,128)S(1)}, u32[]{:S(2)}, u32[]{:S(2)}) %all-to-all-start.5) | async-done | bytes 131104 | tf_op jit(solution)/shard_map/all_to_all | solution.py:214
  141.3 0.0 copy-start.1
  141.3 2.2 %copy-done.1 = bf16[1,1024,2048]{2,1,0:T(8,128)(2,1)S(1)} copy-done((bf16[1,1024,2048]{2,1,0:T(8,128)(2,1)S(1)}, bf16[1,1024,2048]{2,1,0:T(8,128)(2,1)}, u32[]{:S(2)}) %copy-start.1) | copy-done | bytes 4194328
  143.5 7.7 %shard_map.75 = (bf16[448,2048]{1,0:T(8,128)(2,1)}, f32[64,448]{1,0:T(8,128)}) custom-call(f32[4,64,128]{2,1,0:T(8,128)S(1)} %bitcast.42, f32[16,64,128]{2,1,0:T(8,128)S(1)} %shard_map.72.p_ref, bf16[448,1024]{1,0:T(8,128)(2,1)S(1)} %bitcast.32, bf16[1024,2048]{1,0:T(8,128)(2,1)S(1)} %bitcast.26, bf16[448,2048]{1,0:T(8,128)(2,1)S(1)} %bitcast.29), custom_call_target="tpu_custom_call" | custom-call | tf_op jit(solution)/shard_map/pallas_call | solution.py:47
  (1 shorter events, 0.0 us)
Async XLA Ops:
  7.2 14.6 %copy-start.2 = (bf16[1,2048,448]{1,2,0:T(8,128)(2,1)S(1)}, bf16[1,2048,448]{1,2,0:T(8,128)(2,1)}, u32[]{:S(2)}) copy-start(bf16[1,2048,448]{1,2,0:T(8,128)(2,1)} %param.6) | copy-start | bytes 5505028
  7.2 100.6 %all-gather.3.cloned.1.call-start = ((), (), s32[]{:S(2)}) async-start(), calls=%async_computation.6 | async-start | bytes 4456448 | tf_op jit(solution)/shard_map/all_gather | solution.py:174
  7.9 1.2 copy-start.3
  9.1 0.9 copy-start.6
  10.0 11.7 %copy-start.7 = (f32[448,64]{0,1:T(8,128)S(1)}, f32[448,64]{0,1:T(8,128)}, u32[]{:S(2)}) copy-start(f32[448,64]{0,1:T(8,128)} %param.7) | copy-start | bytes 344068
  11.2 21.7 %copy-start.5 = (bf16[1,64,2048]{2,1,0:T(8,128)(2,1)S(1)}, bf16[1,64,2048]{2,1,0:T(8,128)(2,1)}, u32[]{:S(2)}) copy-start(bf16[1,64,2048]{2,1,0:T(8,128)(2,1)} %param.4) | copy-start | bytes 786436
  11.2 21.7 %all-to-all-start = ((f32[16,32,128]{2,1,0:T(8,128)}), f32[16,32,128]{2,1,0:T(8,128)S(1)}, u32[]{:S(2)}, u32[]{:S(2)}) async-start(f32[16,32,128]{2,1,0:T(8,128)} %shard_map.67), calls=%async_computation | async-start | bytes 524288 | tf_op jit(solution)/shard_map/all_to_all | solution.py:176
  37.9 69.9 %copy-start.4 = (bf16[1,1024,448]{1,2,0:T(8,128)(2,1)S(1)}, bf16[1,1024,448]{1,2,0:T(8,128)(2,1)}, u32[]{:S(2)}) copy-start(bf16[1,1024,448]{1,2,0:T(8,128)(2,1)} %param.5) | copy-start | bytes 2752516
  92.7 3.4 %collective-permute-start = (f32[8,64,128]{2,1,0:T(8,128)S(1)}, f32[8,64,128]{2,1,0:T(8,128)S(1)}, u32[]{:S(2)}, u32[]{:S(2)}) collective-permute-start(f32[8,64,128]{2,1,0:T(8,128)S(1)} %bitcast.38), channel_id=1, source_target_pairs={{0,1},{1,0},{2,3},{3,2},{4,5},{5,4},{6,7},{7,6},{8,9},{9,8},{10,11... | collective-permute-start | bytes 786440 | tf_op jit(solution)/shard_map/ppermute | solution.py:191
  96.1 0.7 copy-start.8
  96.8 0.9 copy-start.9
  107.8 2.2 %copy-start = (bf16[1,1024,2048]{2,1,0:T(8,128)(2,1)S(1)}, bf16[1,1024,2048]{2,1,0:T(8,128)(2,1)}, u32[]{:S(2)}) copy-start(bf16[1,1024,2048]{2,1,0:T(8,128)(2,1)} %all-gather.3.cloned.1.call-done) | copy-start | bytes 12582916
  127.1 14.2 %all-to-all-start.5 = ((f32[32,8,128]{2,1,0:T(8,128)}), f32[32,8,128]{2,1,0:T(8,128)S(1)}, u32[]{:S(2)}, u32[]{:S(2)}) async-start(f32[32,8,128]{2,1,0:T(8,128)} %shard_map.74), calls=%async_computation.5 | async-start | bytes 262144 | tf_op jit(solution)/shard_map/all_to_all | solution.py:214
  141.3 2.2 %copy-start.1 = (bf16[1,1024,2048]{2,1,0:T(8,128)(2,1)S(1)}, bf16[1,1024,2048]{2,1,0:T(8,128)(2,1)}, u32[]{:S(2)}) copy-start(bf16[1,1024,2048]{2,1,0:T(8,128)(2,1)} %all-gather.3.cloned.1.call-done) | copy-start | bytes 12582916
Sparse Core Ops, SparseCore 0:
  10.1 52.7 all-gather.2

commit v2 on v1

v2 whole, which is shorter than its diff:
```python
import jax
import jax.numpy as jnp
from jax import lax
from jax.experimental import pallas as pl
from jax.experimental.pallas import tpu as pltpu
from jax.sharding import Mesh
from jax.sharding import PartitionSpec as P

LANES = 128
SUBLANES = 8
EPS = 1e-06
BF16 = jnp.bfloat16
F32 = jnp.float32


def split3(value):
    high = value.astype(BF16)
    rest = value - high.astype(F32)
    middle = rest.astype(BF16)
    low = (rest - middle.astype(F32)).astype(BF16)
    return high, middle, low


def stacked(value):
    return jnp.concatenate(split3(value), axis=0)


def unstacked(value):
    rows = value.shape[0] // 3
    return (value[2 * rows :] + value[rows : 2 * rows]) + value[:rows]


def exact_dot(value, exact):
    return unstacked(jnp.dot(stacked(value), exact, preferred_element_type=F32))


def exact_dot_t(value, exact):
    return unstacked(
        lax.dot_general(
            stacked(value), exact, (((1,), (1,)), ((), ())), preferred_element_type=F32
        )
    )


def call(kernel, out_shape, *args, grid=None, vmem=12, **kw):
    shapes = jax.tree.map(lambda s: jax.ShapeDtypeStruct(*s), out_shape, is_leaf=lambda s: isinstance(s, tuple) and isinstance(s[0], tuple))
    return pl.pallas_call(
        kernel,
        out_shape=shapes,
        compiler_params=pltpu.CompilerParams(vmem_limit_bytes=vmem * 2**20),
        **({} if grid is None else {"grid": grid}),
        **kw,
    )(*args)


def started(sources, targets, sems):
    copies = [pltpu.make_async_copy(*pair, sems.at[i]) for i, pair in enumerate(zip(sources, targets))]
    for copy in copies:
        copy.start()
    return copies


def fetched(sources, targets, sems):
    for copy in started(sources, targets, sems):
        copy.wait()


def cotangent_kernel(q_hbm, g_hbm, out_ref, q_ref, g_ref, sems):
    fetched((q_hbm, g_hbm), (q_ref, g_ref), sems)
    rank = q_ref.shape[0]
    half = rank // 2
    product = exact_dot(q_ref[...], g_ref[...])
    low = lax.broadcasted_iota(jnp.int32, (half, LANES), 1) < LANES // 2
    for tile in range(product.shape[1] // LANES):
        block = product[:, tile * LANES : (tile + 1) * LANES]
        top, bottom = block[:half], block[half:]
        out_ref[2 * tile] = jnp.where(low, top, pltpu.roll(bottom, LANES // 2, 1))
        out_ref[2 * tile + 1] = jnp.where(low, pltpu.roll(top, LANES // 2, 1), bottom)


def feedback_kernel(q_ref, f_ref, out_ref):
    product = exact_dot(q_ref[...], f_ref[...])
    for tile in range(out_ref.shape[0]):
        out_ref[tile] = product[:, tile * LANES : (tile + 1) * LANES]


def left_kernel(y_ref, a_ref, pf_ref, out_ref):
    total = y_ref[0]
    for source in range(1, y_ref.shape[0]):
        total = total + y_ref[source]
    tokens = a_ref.shape[0]
    mine = jnp.concatenate([total[:, :tokens], total[:, tokens:]], axis=0)
    product = exact_dot(mine, a_ref[...])
    for tile in range(out_ref.shape[0]):
        out_ref[tile] = product[:, tile * LANES : (tile + 1) * LANES] + pf_ref[tile]


def pair_kernel(x_ref, out_ref):
    out_ref[...] = x_ref[0] + x_ref[1]


def share_kernel(scale, x_ref, out_ref):
    total = x_ref[0]
    for source in range(1, x_ref.shape[0]):
        total = total + x_ref[source]
    total = total * scale
    for target in range(out_ref.shape[0]):
        out_ref[target] = total


def share(x, targets, scale):
    return call(lambda *refs: share_kernel(scale, *refs), ((targets,) + x.shape[1:], F32), x)


def tree_sum(values):
    while len(values) > 1:
        values = [sum(values[i : i + 2]) for i in range(0, len(values), 2)]
    return values[0]


def lane_sum(values):
    return jnp.sum(tree_sum(values), axis=1, keepdims=True)


def orthonormal(x_ref):
    tiles, rank, _ = x_ref.shape
    index = lax.broadcasted_iota(jnp.int32, (SUBLANES, 1), 0)
    for first in range(0, rank, SUBLANES):
        group = [x_ref[tile, first : first + SUBLANES, :] for tile in range(tiles)]
        squares = jnp.ones((SUBLANES, 1), F32)
        for position in range(SUBLANES):
            rows = [value[position : position + 1, :] for value in group]
            dots = lane_sum([value * row for value, row in zip(group, rows)])
            square = dots[position : position + 1, :] + EPS
            squares = jnp.where(index == position, square, squares)
            if position + 1 < SUBLANES:
                factor = jnp.where(index > position, dots / square, 0.0)
                group = [value - row * factor for value, row in zip(group, rows)]
        scale = 1.0 / jnp.sqrt(squares)
        group = [value * scale for value in group]
        for tile in range(tiles):
            x_ref[tile, first : first + SUBLANES, :] = group[tile]
        if first + SUBLANES == rank:
            break
        overlaps = [
            lane_sum([value * value[position : position + 1, :] for value in group])
            for position in range(SUBLANES - 1)
        ]
        for later in range(first + SUBLANES, rank, SUBLANES):
            values = [x_ref[tile, later : later + SUBLANES, :] for tile in range(tiles)]
            factors = []
            for position in range(SUBLANES):
                row = first + position
                factor = lane_sum([values[tile] * x_ref[tile, row : row + 1, :] for tile in range(tiles)])
                for before in range(position):
                    factor = factor - factors[before] * overlaps[before][position : position + 1, :]
                factors.append(factor)
            for tile in range(tiles):
                change = tree_sum(
                    [x_ref[tile, first + i : first + i + 1, :] * factors[i] for i in range(SUBLANES)]
                )
                x_ref[tile, later : later + SUBLANES, :] = values[tile] - change


def wide(p_ref):
    return jnp.concatenate([p_ref[tile] for tile in range(p_ref.shape[0])], axis=1)


def pair_dot_t(value, exact):
    rows = value.shape[0]
    high, middle, _ = split3(value)
    product = lax.dot_general(
        jnp.concatenate([high, middle], axis=0),
        exact,
        (((1,), (1,)), ((), ())),
        preferred_element_type=F32,
    )
    return product[rows:] + product[:rows]


def factors_kernel(
    place_ref, mine_hbm, other_hbm, a_hbm, f_hbm, g_hbm,
    p_hbm, p_mine_ref, out_ref,
    p_ref, a_ref, f_ref, g_ref, sems,
):
    tiles = p_ref.shape[0]
    part = tiles // 2
    member, core = place_ref[0], place_ref[1]
    mine, other = p_ref.at[pl.ds(core * part, part)], p_ref.at[pl.ds((1 - core) * part, part)]
    copies = started((mine_hbm, other_hbm, a_hbm, f_hbm, g_hbm), (mine, other, a_ref, f_ref, g_ref), sems)
    copies[0].wait()
    copies[1].wait()
    orthonormal(p_ref)
    written = pltpu.make_async_copy(p_ref, p_hbm, sems.at[0])
    written.start()
    p_mine_ref[...] = p_ref[member]
    p = wide(p_ref)
    for copy in copies[2:]:
        copy.wait()
    product = pair_dot_t(p, f_ref[...])
    product = product + pair_dot_t(pair_dot_t(p, a_ref[...]), g_ref[...])
    width = product.shape[1]
    for tile in range(out_ref.shape[0]):
        block = product[:, tile * LANES : min(width, (tile + 1) * LANES)]
        if block.shape[1] < LANES:
            block = jnp.concatenate([block, jnp.zeros((block.shape[0], LANES - block.shape[1]), F32)], axis=1)
        out_ref[tile] = block
    written.wait()


def corrected_kernel(a_ref, g_ref, f_ref, out_ref):
    product = jnp.dot(g_ref[...], a_ref[...], preferred_element_type=F32)
    out_ref[...] = product + f_ref[...].astype(F32)


def feedback_out_kernel(q_hbm, p_hbm, c_hbm, fb_hbm, qt_ref, q_ref, p_ref, c_ref, fb_ref, sems, c_sems, fb_sems):
    steps = c_sems.shape[0]
    step = c_ref.shape[1] // steps
    copies = started((q_hbm, p_hbm), (q_ref, p_ref), sems)
    slices = [pl.ds(i * step, step) for i in range(steps)]
    reads = started([c_hbm.at[:, at] for at in slices], [c_ref.at[:, at] for at in slices], c_sems)
    writes = [
        pltpu.make_async_copy(fb_ref.at[:, at], fb_hbm.at[:, at], fb_sems.at[i]) for i, at in enumerate(slices)
    ]
    copies[0].wait()
    q_wide = wide(q_ref)[:, : qt_ref.shape[1]]
    qt_ref[...] = q_wide
    q1, q2, _ = split3(q_wide.T)
    left = jnp.concatenate([q2, q2, q1, q1], axis=1)
    copies[1].wait()
    for i, at in enumerate(slices):
        p1, p2, _ = split3(jnp.concatenate([p_ref[t] for t in range(i * step // LANES, (i + 1) * step // LANES)], axis=1))
        right = jnp.concatenate([p2, p1, p2, p1], axis=0)
        low_rank = jnp.dot(left, right, preferred_element_type=F32)
        reads[i].wait()
        fb_ref[:, at] = (c_ref[:, at] - low_rank).astype(BF16)
        writes[i].start()
    for write in writes:
        write.wait()


def body(activations, out_grad, feedback, q_prev):
    xy, tensor = ("x", "y"), ("z", "c")
    a = activations[0]
    gt = out_grad[0].T
    ft = feedback[0].T
    qt = q_prev.T
    width, columns = ft.shape[1], ft.shape[0]
    rank, tokens = qt.shape[0], gt.shape[1]
    replicas = lax.axis_size(xy)
    members = lax.axis_size(tensor)
    tiles = width // LANES

    swap = [(0, 1), (1, 0)]
    vmem = pl.BlockSpec(memory_space=pltpu.VMEM)
    smem = pl.BlockSpec(memory_space=pltpu.SMEM)
    anywhere = pl.BlockSpec(memory_space=pl.ANY)

    y = call(
        cotangent_kernel,
        ((members, rank // 2, LANES), F32),
        qt,
        gt,
        in_specs=[anywhere, anywhere],
        out_specs=vmem,
        scratch_shapes=[pltpu.VMEM(qt.shape, F32), pltpu.VMEM(gt.shape, BF16), pltpu.SemaphoreType.DMA((2,))],
        vmem=57,
    )
    y = lax.all_to_all(y, tensor, 0, 0)
    a_full = lax.all_gather(a, tensor, axis=0, tiled=True)
    layers = lax.axis_size("z")

    p_feedback = call(feedback_kernel, ((tiles, rank, LANES), F32), qt, ft)
    p = call(left_kernel, ((tiles, rank, LANES), F32), y, a, p_feedback)

    p = lax.all_to_all(p.reshape(2, tiles // 2 * rank, LANES), "c", 0, 0)
    p = call(pair_kernel, ((tiles // 2 * rank, LANES), F32), p)
    p = lax.all_to_all(p.reshape(replicas, -1, LANES), xy, 0, 0)
    p = share(p, layers, 1.0 / replicas)
    p = lax.all_to_all(p, "z", 0, 0)
    p = share(p, replicas, 1.0)
    p = lax.all_to_all(p, xy, 0, 0).reshape(tiles // 2, rank, LANES)

    rows = columns // 4
    block = pl.BlockSpec((rows, width), lambda i: (i, 0))
    corrected = call(
        corrected_kernel,
        ((columns, width), F32),
        a_full,
        gt,
        ft,
        grid=(columns // rows,),
        in_specs=[
            pl.BlockSpec((tokens, width), lambda i: (0, 0)),
            pl.BlockSpec((rows, tokens), lambda i: (i, 0)),
            block,
        ],
        out_specs=block,
        vmem=57,
        cost_estimate=pl.CostEstimate(
            flops=2 * columns * width * tokens, bytes_accessed=12 * 2**20, transcendentals=0
        ),
    )
    p, corrected = lax.optimization_barrier((p, corrected))

    p_other = lax.ppermute(p, "c", swap)
    q_tiles = -(-columns // LANES)
    place = jnp.stack([lax.axis_index(tensor), lax.axis_index("c")]).astype(jnp.int32)
    p_orth, p_mine, q = call(
        factors_kernel,
        [((tiles, rank, LANES), F32), ((rank, LANES), F32), ((q_tiles, rank, LANES), F32)],
        place,
        p,
        p_other,
        a_full,
        ft,
        gt,
        in_specs=[smem] + [anywhere] * 5,
        out_specs=[anywhere, vmem, vmem],
        scratch_shapes=[
            pltpu.VMEM((tiles, rank, LANES), F32),
            pltpu.VMEM(a_full.shape, BF16),
            pltpu.VMEM(ft.shape, BF16),
            pltpu.VMEM(gt.shape, BF16),
            pltpu.SemaphoreType.DMA((5,)),
        ],
        vmem=57,
    )

    q = lax.all_to_all(q.reshape(replicas, -1, LANES), xy, 0, 0)
    q = share(q, replicas, 1.0 / replicas)
    q = lax.all_to_all(q, xy, 0, 0).reshape(q_tiles, rank, LANES)

    steps = 4
    fbt, q_new = call(
        feedback_out_kernel,
        [((columns, width), BF16), ((rank, columns), F32)],
        q,
        p_orth,
        corrected,
        in_specs=[anywhere] * 3,
        out_specs=[anywhere, vmem],
        scratch_shapes=[
            pltpu.VMEM(q.shape, F32),
            pltpu.VMEM(p_orth.shape, F32),
            pltpu.VMEM(corrected.shape, F32),
            pltpu.VMEM(corrected.shape, BF16),
            pltpu.SemaphoreType.DMA((2,)),
            pltpu.SemaphoreType.DMA((steps,)),
            pltpu.SemaphoreType.DMA((steps,)),
        ],
        vmem=57,
    )
    return fbt.T[None], p_mine.T, q_new.T


def solution(mesh):
    sizes = (4, 8, 8, 2)
    fine = Mesh(mesh.devices.reshape(sizes), ("x", "y", "z", "c"))
    dp, tensor = ("x", "y"), ("z", "c")
    in_specs = (
        P(dp, tensor, None),
        P(dp, None, tensor),
        P(dp, None, tensor),
        P(tensor, None),
    )
    out_specs = (P(dp, None, tensor), P(tensor, None), P(tensor, None))
    return jax.shard_map(body, mesh=fine, in_specs=in_specs, out_specs=out_specs, check_vma=False)
```

time: 159 us -> 146 us (0.918)
  waiting for transfers between devices: 22 us -> 13.6 us
  Pallas kernels: 22.9 us -> 29.1 us
  local copies, waits for them, and re-layouts: 8.74 us -> 3.13 us
  blocking collectives: 73.3 us -> 68.4 us
    pallas_call x9 -> x10, Pallas kernels: 22.9 us -> 29.1 us  [call(): pl.pallas_call(kernel, out_shape=shapes, compiler_params=pltpu.CompilerPa...]
    all_to_all x1, waiting for transfers between devices: 9.24 us -> 3.75 us  [body(): p = lax.all_to_all(p, xy, 0, 0).reshape(tiles // 2, rank, LANES)]
    all_to_all x3 -> x4, blocking collectives: 68.7 us -> 63.7 us  [the longest x1 22.6 us: body(): p = lax.all_to_all(p.reshape(replicas, -1, LANES), xy, 0, 0)]
    unnamed x20 -> x10, local copies, waits for them, and re-layouts: 8.11 us -> 3.13 us
    all_to_all x1, waiting for transfers between devices: 10.6 us -> 8.2 us  [body(): y = lax.all_to_all(y, tensor, 0, 0)]
where the time goes in v2:
time: 146 us
  blocking collectives  68.4 us (47%)
  Pallas kernels  29.1 us (20%)
  starting transfers between devices  16.9 us (12%)
  between operations  14.1 us (10%)
  waiting for transfers between devices  13.6 us (9%)
  local copies, waits for them, and re-layouts  3.13 us (2%)
    pallas_call x10, Pallas kernels, call(): pl.pallas_call(kernel, out_shape=shapes, compiler_params=pltpu.CompilerPa...  29.1 us
    all_to_all x1, blocking collectives, body(): p = lax.all_to_all(p.reshape(replicas, -1, LANES), xy, 0, 0)  22.6 us
    all_to_all x1, blocking collectives, body(): q = lax.all_to_all(q.reshape(replicas, -1, LANES), xy, 0, 0)  16.1 us
    all_to_all x1, blocking collectives, body(): q = lax.all_to_all(q, xy, 0, 0).reshape(q_tiles, rank, LANES)  14 us
    all_to_all x1, blocking collectives, body(): p = lax.all_to_all(p, 'z', 0, 0)  11 us
    all_to_all x1, starting transfers between devices, body(): y = lax.all_to_all(y, tensor, 0, 0)  10.4 us
    all_to_all x1, waiting for transfers between devices, body(): y = lax.all_to_all(y, tensor, 0, 0)  8.2 us
    all_to_all x1, blocking collectives, body(): p = lax.all_to_all(p.reshape(2, tiles // 2 * rank, LANES), 'c', 0, 0)  4.69 us
  transfers between devices with their start and end apart: 4, of which 3 were waited for; matrix products, arithmetic and copies ran while one was open for 0% of the time, Pallas kernels for 8%

profile of v2, /device:TPU:8, one launch (start us, length us, event | category | flops | bytes accessed | tf_op | source)
XLA Modules:
  0.0 145.8 jit_solution(14372074369242095450)
XLA Ops:
  7.2 0.0 copy-start.1
  7.2 0.0 all-gather.3.cloned.1.call-start
  7.2 0.7 all-gather.3.cloned.1.call-update
  7.9 2.4 %shard_map.67 = f32[16,32,128]{2,1,0:T(8,128)} custom-call(f32[64,448]{1,0:T(8,128)} %bitcast.27, bf16[448,1024]{1,0:T(8,128)(2,1)} %bitcast.31), custom_call_target="tpu_custom_call" | custom-call | tf_op jit(solution)/shard_map/pallas_call | solution.py:47
  10.4 10.4 %all-to-all-start = ((f32[16,32,128]{2,1,0:T(8,128)}), f32[16,32,128]{2,1,0:T(8,128)S(1)}, u32[]{:S(2)}, u32[]{:S(2)}) async-start(f32[16,32,128]{2,1,0:T(8,128)} %shard_map.67), calls=%async_computation | async-start | bytes 524288 | tf_op jit(solution)/shard_map/all_to_all | solution.py:269
  20.8 0.0 copy-start
  20.8 1.5 %copy-done = bf16[1,2048,448]{1,2,0:T(8,128)(2,1)S(1)} copy-done((bf16[1,2048,448]{1,2,0:T(8,128)(2,1)S(1)}, bf16[1,2048,448]{1,2,0:T(8,128)(2,1)}, u32[]{:S(2)}) %copy-start) | copy-done | bytes 1835032
  22.3 0.0 copy-start.2
  22.3 0.9 copy-done.2
  23.2 0.6 shard_map.68.pf_ref
  23.8 8.2 %all-to-all-done.y_ref = f32[16,32,128]{2,1,0:T(8,128)S(1)} async-done(((f32[16,32,128]{2,1,0:T(8,128)}), f32[16,32,128]{2,1,0:T(8,128)S(1)}, u32[]{:S(2)}, u32[]{:S(2)}) %all-to-all-start) | async-done | bytes 262176 | tf_op jit(solution)/shard_map/all_to_all | solution.py:269
  32.0 0.0 copy-done.1
  32.0 0.4 shard_map.69
  32.4 4.7 %all_to_all.35.x_ref = f32[2,512,128]{2,1,0:T(8,128)S(1)} all-to-all(f32[2,512,128]{2,1,0:T(8,128)S(1)} %bitcast.24), channel_id=1, replica_groups=mesh['x'=4,'y'=8,'z'=8,'c'=2] {'c'}, dimensions={0} | all-to-all | bytes 1048576 | tf_op jit(solution)/shard_map/all_to_all | solution.py:276
  37.1 22.6 %all_to_all.36.refs_0_ = f32[32,16,128]{2,1,0:T(8,128)S(1)} all-to-all(f32[32,16,128]{2,1,0:T(8,128)S(1)} %bitcast.25), channel_id=1, replica_groups=mesh['x'=4,'y'=8,'z'=8,'c'=2] {'x','y'}, dimensions={0} | all-to-all | bytes 524288 | tf_op jit(solution)/shard_map/all_to_all | solution.py:278
  59.7 11.0 %all_to_all.37.refs_0_ = f32[8,16,128]{2,1,0:T(8,128)S(1)} all-to-all(f32[8,16,128]{2,1,0:T(8,128)S(1)} %shard_map.71), channel_id=1, replica_groups=mesh['x'=4,'y'=8,'z'=8,'c'=2] {'z'}, dimensions={0} | all-to-all | bytes 131072 | tf_op jit(solution)/shard_map/all_to_all | solution.py:280
  70.8 0.7 shard_map.72
  71.5 4.6 %all-to-all-start.4 = ((f32[32,16,128]{2,1,0:T(8,128)}), f32[32,16,128]{2,1,0:T(8,128)S(1)}, u32[]{:S(2)}, u32[]{:S(2)}) async-start(f32[32,16,128]{2,1,0:T(8,128)} %shard_map.72), calls=%async_computation.4 | async-start | bytes 524288 | tf_op jit(solution)/shard_map/all_to_all | solution.py:282
  76.1 0.0 all-gather.3.cloned.1.call-done
  76.1 7.3 %shard_map.73.c_hbm = f32[448,2048]{1,0:T(8,128)} custom-call(bf16[1024,2048]{1,0:T(8,128)(2,1)} %bitcast.29, bf16[448,1024]{1,0:T(8,128)(2,1)} %bitcast.32, bf16[448,2048]{1,0:T(8,128)(2,1)} %bitcast.21), custom_call_target="tpu_custom_call" | custom-call | flops 1879048192 | bytes 12582912 | tf_op jit(solution)/shard_map/pallas_call | solution.py:47
  83.4 3.7 %all-to-all-done.4 = f32[32,16,128]{2,1,0:T(8,128)S(1)} async-done(((f32[32,16,128]{2,1,0:T(8,128)}), f32[32,16,128]{2,1,0:T(8,128)S(1)}, u32[]{:S(2)}, u32[]{:S(2)}) %all-to-all-start.4) | async-done | bytes 262176 | tf_op jit(solution)/shard_map/all_to_all | solution.py:282
  87.1 0.0 copy-start.3
  87.1 1.9 %collective-permute-start = (f32[8,64,128]{2,1,0:T(8,128)S(1)}, f32[8,64,128]{2,1,0:T(8,128)S(1)}, u32[]{:S(2)}, u32[]{:S(2)}) collective-permute-start(f32[8,64,128]{2,1,0:T(8,128)S(1)} %bitcast.34), channel_id=1, source_target_pairs={{0,1},{1,0},{2,3},{3,2},{4,5},{5,4},{6,7},{7,6},{8,9},{9,8},{10,11... | collective-permute-start | bytes 786440 | tf_op jit(solution)/shard_map/ppermute | solution.py:306
  89.0 0.6 pad_add_fusion.place_ref
  89.6 0.9 collective-permute-done.other_hbm
  90.5 0.0 copy-done.3
  90.5 0.0 copy-start.4
  90.5 0.7 copy-done.4
  91.3 12.8 %shard_map.74 = (f32[16,64,128]{2,1,0:T(8,128)}, f32[64,128]{1,0:T(8,128)}, f32[4,64,128]{2,1,0:T(8,128)}) custom-call(s32[2]{0:T(128)} %pad_add_fusion.place_ref, f32[8,64,128]{2,1,0:T(8,128)} %bitcast.35, f32[8,64,128]{2,1,0:T(8,128)} %copy-done.4, bf16[1024,2048]{1,0:T(8,128)(2,1)} %bitcast.30, bf16[448,2048]{1,0:T(8,128)(2,1)} %bitcast.22, ...), custom_call_target="tpu_custom_call" | custom-call | tf_op jit(solution)/shard_map/pallas_call | solution.py:47
  104.0 16.1 %all_to_all.38.refs_0_ = f32[32,8,128]{2,1,0:T(8,128)S(1)} all-to-all(f32[32,8,128]{2,1,0:T(8,128)} %bitcast.37), channel_id=1, replica_groups=mesh['x'=4,'y'=8,'z'=8,'c'=2] {'x','y'}, dimensions={0} | all-to-all | bytes 262144 | tf_op jit(solution)/shard_map/all_to_all | solution.py:330
  120.1 14.0 %all_to_all.39 = f32[32,8,128]{2,1,0:T(8,128)} all-to-all(f32[32,8,128]{2,1,0:T(8,128)S(1)} %shard_map.75), channel_id=1, replica_groups=mesh['x'=4,'y'=8,'z'=8,'c'=2] {'x','y'}, dimensions={0} | all-to-all | bytes 262144 | tf_op jit(solution)/shard_map/all_to_all | solution.py:332
  134.2 4.8 %shard_map.76 = (bf16[448,2048]{1,0:T(8,128)(2,1)}, f32[64,448]{1,0:T(8,128)}) custom-call(f32[4,64,128]{2,1,0:T(8,128)} %bitcast.36, f32[16,64,128]{2,1,0:T(8,128)} %get-tuple-element.12.p_hbm, f32[448,2048]{1,0:T(8,128)} %shard_map.73.c_hbm), custom_call_target="tpu_custom_call" | custom-call | tf_op jit(solution)/shard_map/pallas_call | solution.py:47
  (3 shorter events, 0.1 us)
Async XLA Ops:
  7.2 24.8 %copy-start.1 = (bf16[1,64,2048]{2,1,0:T(8,128)(2,1)S(1)}, bf16[1,64,2048]{2,1,0:T(8,128)(2,1)}, u32[]{:S(2)}) copy-start(bf16[1,64,2048]{2,1,0:T(8,128)(2,1)} %param.4) | copy-start | bytes 786436
  7.2 68.9 %all-gather.3.cloned.1.call-start = ((), (), s32[]{:S(2)}) async-start(), calls=%async_computation.7 | async-start | bytes 4456448 | tf_op jit(solution)/shard_map/all_gather | solution.py:270
  10.4 21.6 %all-to-all-start = ((f32[16,32,128]{2,1,0:T(8,128)}), f32[16,32,128]{2,1,0:T(8,128)S(1)}, u32[]{:S(2)}, u32[]{:S(2)}) async-start(f32[16,32,128]{2,1,0:T(8,128)} %shard_map.67), calls=%async_computation | async-start | bytes 524288 | tf_op jit(solution)/shard_map/all_to_all | solution.py:269
  20.8 1.5 %copy-start = (bf16[1,2048,448]{1,2,0:T(8,128)(2,1)S(1)}, bf16[1,2048,448]{1,2,0:T(8,128)(2,1)}, u32[]{:S(2)}) copy-start(bf16[1,2048,448]{1,2,0:T(8,128)(2,1)} %param.6) | copy-start | bytes 5505028
  22.3 0.9 copy-start.2
  71.5 15.6 %all-to-all-start.4 = ((f32[32,16,128]{2,1,0:T(8,128)}), f32[32,16,128]{2,1,0:T(8,128)S(1)}, u32[]{:S(2)}, u32[]{:S(2)}) async-start(f32[32,16,128]{2,1,0:T(8,128)} %shard_map.72), calls=%async_computation.4 | async-start | bytes 524288 | tf_op jit(solution)/shard_map/all_to_all | solution.py:282
  87.1 3.4 %copy-start.3 = (f32[32,16,128]{2,1,0:T(8,128)}, f32[32,16,128]{2,1,0:T(8,128)S(1)}, u32[]{:S(2)}) copy-start(f32[32,16,128]{2,1,0:T(8,128)S(1)} %all-to-all-done.4) | copy-start | bytes 786436
  87.1 3.4 %collective-permute-start = (f32[8,64,128]{2,1,0:T(8,128)S(1)}, f32[8,64,128]{2,1,0:T(8,128)S(1)}, u32[]{:S(2)}, u32[]{:S(2)}) collective-permute-start(f32[8,64,128]{2,1,0:T(8,128)S(1)} %bitcast.34), channel_id=1, source_target_pairs={{0,1},{1,0},{2,3},{3,2},{4,5},{5,4},{6,7},{7,6},{8,9},{9,8},{10,11... | collective-permute-start | bytes 786440 | tf_op jit(solution)/shard_map/ppermute | solution.py:306
  90.5 0.7 copy-start.4
Sparse Core Ops, SparseCore 0:
  10.1 50.2 all-gather.2

commit v3 on v2

--- a/solution.py
+++ b/solution.py
@@ -9,6 +9,7 @@
 LANES = 128
 SUBLANES = 8
 EPS = 1e-06
+KEPT = 1 / 32
 BF16 = jnp.bfloat16
 F32 = jnp.float32
 
@@ -60,13 +61,9 @@
     return copies
 
 
-def fetched(sources, targets, sems):
-    for copy in started(sources, targets, sems):
+def cotangent_kernel(q_hbm, g_hbm, out_ref, q_ref, g_ref, sems):
+    for copy in started((q_hbm, g_hbm), (q_ref, g_ref), sems):
         copy.wait()
-
-
-def cotangent_kernel(q_hbm, g_hbm, out_ref, q_ref, g_ref, sems):
-    fetched((q_hbm, g_hbm), (q_ref, g_ref), sems)
     rank = q_ref.shape[0]
     half = rank // 2
     product = exact_dot(q_ref[...], g_ref[...])
@@ -122,44 +119,79 @@
     return jnp.sum(tree_sum(values), axis=1, keepdims=True)
 
 
-def orthonormal(x_ref):
+def sweeps(x_ref):
     tiles, rank, _ = x_ref.shape
+    for first in range(0, rank, SUBLANES):
+
+        def sweep(step, carry, first=first):
+            position = first + step
+            rows = [x_ref[tile, pl.ds(position, 1), :] for tile in range(tiles)]
+            dots = lane_sum([x_ref[tile, first:, :] * rows[tile] for tile in range(tiles)])
+            square = lane_sum([row * row for row in rows]) + EPS
+            order = lax.broadcasted_iota(jnp.int32, dots.shape, 0) + first
+            factor = jnp.where(order > position, dots / square, 0.0)
+            scale = jnp.where(order == position, 1.0 / jnp.sqrt(square), 1.0)
+            for tile in range(tiles):
+                x_ref[tile, first:, :] = x_ref[tile, first:, :] * scale - rows[tile] * factor
+            return carry
+
+        lax.fori_loop(0, SUBLANES, sweep, 0)
+
+
+def sweep_group(group):
     index = lax.broadcasted_iota(jnp.int32, (SUBLANES, 1), 0)
+    dots = [lane_sum([value * value[i : i + 1, :] for value in group]) for i in range(SUBLANES)]
+    least = [dots[i][i : i + 1, :] * KEPT for i in range(SUBLANES)]
+    squares = jnp.ones((SUBLANES, 1), F32)
+    lost = jnp.zeros((1, 1), F32)
+    factors = []
+    for i in range(SUBLANES):
+        raw = dots[i][i : i + 1, :]
+        square = raw + EPS
+        lost = jnp.where(raw < least[i], 1.0, lost)
+        squares = jnp.where(index == i, square, squares)
+        if i + 1 < SUBLANES:
+            factor = jnp.where(index > i, dots[i] * (1.0 / square), 0.0)
+            factors.append(factor)
+            for j in range(i + 1, SUBLANES):
+                mine = factor[j : j + 1, :]
+                dots[j] = dots[j] - factor * (dots[i][j : j + 1, :] - mine * raw) - mine * dots[i]
+    for i, factor in enumerate(factors):
+        group = [value - value[i : i + 1, :] * factor for value in group]
+    scale = 1.0 / jnp.sqrt(squares)
+    return [value * scale for value in group], lost
+
+
+def orthonormal(x_ref, kept_ref):
+    tiles, rank, _ = x_ref.shape
+    lost = jnp.zeros((1, 1), F32)
     for first in range(0, rank, SUBLANES):
-        group = [x_ref[tile, first : first + SUBLANES, :] for tile in range(tiles)]
-        squares = jnp.ones((SUBLANES, 1), F32)
-        for position in range(SUBLANES):
-            rows = [value[position : position + 1, :] for value in group]
-            dots = lane_sum([value * row for value, row in zip(group, rows)])
-            square = dots[position : position + 1, :] + EPS
-            squares = jnp.where(index == position, square, squares)
-            if position + 1 < SUBLANES:
-                factor = jnp.where(index > position, dots / square, 0.0)
-                group = [value - row * factor for value, row in zip(group, rows)]
-        scale = 1.0 / jnp.sqrt(squares)
-        group = [value * scale for value in group]
+        group, loss = sweep_group([x_ref[tile, first : first + SUBLANES, :] for tile in range(tiles)])
+        lost = jnp.maximum(lost, loss)
         for tile in range(tiles):
             x_ref[tile, first : first + SUBLANES, :] = group[tile]
         if first + SUBLANES == rank:
             break
-        overlaps = [
-            lane_sum([value * value[position : position + 1, :] for value in group])
-            for position in range(SUBLANES - 1)
-        ]
+        overlaps = [lane_sum([value * value[i : i + 1, :] for value in group]) for i in range(SUBLANES - 1)]
         for later in range(first + SUBLANES, rank, SUBLANES):
             values = [x_ref[tile, later : later + SUBLANES, :] for tile in range(tiles)]
             factors = []
-            for position in range(SUBLANES):
-                row = first + position
+            for i in range(SUBLANES):
+                row = first + i
                 factor = lane_sum([values[tile] * x_ref[tile, row : row + 1, :] for tile in range(tiles)])
-                for before in range(position):
-                    factor = factor - factors[before] * overlaps[before][position : position + 1, :]
+                for before in range(i):
+                    factor = factor - factors[before] * overlaps[before][i : i + 1, :]
                 factors.append(factor)
             for tile in range(tiles):
                 change = tree_sum(
                     [x_ref[tile, first + i : first + i + 1, :] * factors[i] for i in range(SUBLANES)]
                 )
                 x_ref[tile, later : later + SUBLANES, :] = values[tile] - change
+
+    @pl.when(jnp.max(lost) > 0.0)
+    def _():
+        x_ref[...] = kept_ref[...]
+        sweeps(x_ref)
 
 
 def wide(p_ref):
@@ -179,23 +211,21 @@
 
 
 def factors_kernel(
-    place_ref, mine_hbm, other_hbm, a_hbm, f_hbm, g_hbm,
-    p_hbm, p_mine_ref, out_ref,
-    p_ref, a_ref, f_ref, g_ref, sems,
+    place_ref, mine_ref, other_ref, a_hbm, f_hbm, g_hbm,
+    p_ref, p_mine_ref, out_ref,
+    kept_ref, a_ref, f_ref, g_ref, sems,
 ):
     tiles = p_ref.shape[0]
     part = tiles // 2
     member, core = place_ref[0], place_ref[1]
-    mine, other = p_ref.at[pl.ds(core * part, part)], p_ref.at[pl.ds((1 - core) * part, part)]
-    copies = started((mine_hbm, other_hbm, a_hbm, f_hbm, g_hbm), (mine, other, a_ref, f_ref, g_ref), sems)
-    copies[0].wait()
-    copies[1].wait()
-    orthonormal(p_ref)
-    written = pltpu.make_async_copy(p_ref, p_hbm, sems.at[0])
-    written.start()
+    copies = started((a_hbm, f_hbm, g_hbm), (a_ref, f_ref, g_ref), sems)
+    for ref in (p_ref, kept_ref):
+        ref[pl.ds(core * part, part)] = mine_ref[...]
+        ref[pl.ds((1 - core) * part, part)] = other_ref[...]
+    orthonormal(p_ref, kept_ref)
     p_mine_ref[...] = p_ref[member]
     p = wide(p_ref)
-    for copy in copies[2:]:
+    for copy in copies:
         copy.wait()
     product = pair_dot_t(p, f_ref[...])
     product = product + pair_dot_t(pair_dot_t(p, a_ref[...]), g_ref[...])
@@ -205,7 +235,6 @@
         if block.shape[1] < LANES:
             block = jnp.concatenate([block, jnp.zeros((block.shape[0], LANES - block.shape[1]), F32)], axis=1)
         out_ref[tile] = block
-    written.wait()
 
 
 def corrected_kernel(a_ref, g_ref, f_ref, out_ref):
@@ -213,28 +242,22 @@
     out_ref[...] = product + f_ref[...].astype(F32)
 
 
-def feedback_out_kernel(q_hbm, p_hbm, c_hbm, fb_hbm, qt_ref, q_ref, p_ref, c_ref, fb_ref, sems, c_sems, fb_sems):
-    steps = c_sems.shape[0]
+def feedback_out_kernel(q_ref, p_ref, c_ref, fb_hbm, qt_ref, fb_ref, fb_sems):
+    steps = fb_sems.shape[0]
     step = c_ref.shape[1] // steps
-    copies = started((q_hbm, p_hbm), (q_ref, p_ref), sems)
-    slices = [pl.ds(i * step, step) for i in range(steps)]
-    reads = started([c_hbm.at[:, at] for at in slices], [c_ref.at[:, at] for at in slices], c_sems)
-    writes = [
-        pltpu.make_async_copy(fb_ref.at[:, at], fb_hbm.at[:, at], fb_sems.at[i]) for i, at in enumerate(slices)
-    ]
-    copies[0].wait()
     q_wide = wide(q_ref)[:, : qt_ref.shape[1]]
     qt_ref[...] = q_wide
     q1, q2, _ = split3(q_wide.T)
     left = jnp.concatenate([q2, q2, q1, q1], axis=1)
-    copies[1].wait()
-    for i, at in enumerate(slices):
+    writes = []
+    for i in range(steps):
+        at = pl.ds(i * step, step)
         p1, p2, _ = split3(jnp.concatenate([p_ref[t] for t in range(i * step // LANES, (i + 1) * step // LANES)], axis=1))
         right = jnp.concatenate([p2, p1, p2, p1], axis=0)
         low_rank = jnp.dot(left, right, preferred_element_type=F32)
-        reads[i].wait()
         fb_ref[:, at] = (c_ref[:, at] - low_rank).astype(BF16)
-        writes[i].start()
+        writes.append(pltpu.make_async_copy(fb_ref.at[:, at], fb_hbm.at[:, at], fb_sems.at[i]))
+        writes[-1].start()
     for write in writes:
         write.wait()
 
@@ -254,20 +277,21 @@
     swap = [(0, 1), (1, 0)]
     vmem = pl.BlockSpec(memory_space=pltpu.VMEM)
     smem = pl.BlockSpec(memory_space=pltpu.SMEM)
-    anywhere = pl.BlockSpec(memory_space=pl.ANY)
+    hbm = pl.BlockSpec(memory_space=pltpu.HBM)
 
     y = call(
         cotangent_kernel,
         ((members, rank // 2, LANES), F32),
         qt,
         gt,
-        in_specs=[anywhere, anywhere],
+        in_specs=[hbm, hbm],
         out_specs=vmem,
         scratch_shapes=[pltpu.VMEM(qt.shape, F32), pltpu.VMEM(gt.shape, BF16), pltpu.SemaphoreType.DMA((2,))],
         vmem=57,
     )
+    a_late, y = lax.optimization_barrier((a, y))
+    a_full = lax.all_gather(a_late, tensor, axis=0, tiled=True)
     y = lax.all_to_all(y, tensor, 0, 0)
-    a_full = lax.all_gather(a, tensor, axis=0, tiled=True)
     layers = lax.axis_size("z")
 
     p_feedback = call(feedback_kernel, ((tiles, rank, LANES), F32), qt, ft)
@@ -315,16 +339,16 @@
         a_full,
         ft,
         gt,
-        in_specs=[smem] + [anywhere] * 5,
-        out_specs=[anywhere, vmem, vmem],
+        in_specs=[smem, vmem, vmem] + [hbm] * 3,
+        out_specs=[vmem] * 3,
         scratch_shapes=[
             pltpu.VMEM((tiles, rank, LANES), F32),
             pltpu.VMEM(a_full.shape, BF16),
             pltpu.VMEM(ft.shape, BF16),
             pltpu.VMEM(gt.shape, BF16),
-            pltpu.SemaphoreType.DMA((5,)),
+            pltpu.SemaphoreType.DMA((3,)),
         ],
-        vmem=57,
+        vmem=54,
     )
 
     q = lax.all_to_all(q.reshape(replicas, -1, LANES), xy, 0, 0)
@@ -338,18 +362,13 @@
         q,
         p_orth,
         corrected,
-        in_specs=[anywhere] * 3,
-        out_specs=[anywhere, vmem],
+        in_specs=[vmem] * 3,
+        out_specs=[hbm, vmem],
         scratch_shapes=[
-            pltpu.VMEM(q.shape, F32),
-            pltpu.VMEM(p_orth.shape, F32),
-            pltpu.VMEM(corrected.shape, F32),
             pltpu.VMEM(corrected.shape, BF16),
-            pltpu.SemaphoreType.DMA((2,)),
-            pltpu.SemaphoreType.DMA((steps,)),
             pltpu.SemaphoreType.DMA((steps,)),
         ],
-        vmem=57,
+        vmem=16,
     )
     return fbt.T[None], p_mine.T, q_new.T
 

time: 146 us -> 141 us (0.966)
  Pallas kernels: 29.1 us -> 23 us
    pallas_call x10, Pallas kernels: 29.1 us -> 23 us  [call(): pl.pallas_call(kernel, out_shape=shapes, compiler_params=pltpu.CompilerPa...]
    unnamed x10 -> x14, local copies, waits for them, and re-layouts: 3.13 us -> 4.19 us
  transfers between devices with their start and end apart: 4 -> 4, of which waited for: 3 -> 3; matrix products, arithmetic and copies ran while one was open for 0% -> 0% of each run, Pallas kernels for 8% -> 6%
where the time goes in v3:
time: 141 us; the launch traced here: 140 us
  blocking collectives  68.2 us (48%)
  Pallas kernels  23 us (16%)
  starting transfers between devices  16.9 us (12%)
  between operations  14.1 us (10%)
  waiting for transfers between devices  12.9 us (9%)
  local copies, waits for them, and re-layouts  4.19 us (3%)
    pallas_call x10, Pallas kernels, call(): pl.pallas_call(kernel, out_shape=shapes, compiler_params=pltpu.CompilerPa...  23 us
    all_to_all x1, blocking collectives, body(): p = lax.all_to_all(p.reshape(replicas, -1, LANES), xy, 0, 0)  22.5 us
    all_to_all x1, blocking collectives, body(): q = lax.all_to_all(q.reshape(replicas, -1, LANES), xy, 0, 0)  16.1 us
    all_to_all x1, blocking collectives, body(): q = lax.all_to_all(q, xy, 0, 0).reshape(q_tiles, rank, LANES)  13.9 us
    all_to_all x1, blocking collectives, body(): p = lax.all_to_all(p, 'z', 0, 0)  11.1 us
    all_to_all x1, starting transfers between devices, body(): y = lax.all_to_all(y, tensor, 0, 0)  10.4 us
    all_to_all x1, waiting for transfers between devices, body(): y = lax.all_to_all(y, tensor, 0, 0)  8.19 us
    all_to_all x1, blocking collectives, body(): p = lax.all_to_all(p.reshape(2, tiles // 2 * rank, LANES), 'c', 0, 0)  4.69 us
  transfers between devices with their start and end apart: 4, of which 3 were waited for; matrix products, arithmetic and copies ran while one was open for 0% of the time, Pallas kernels for 6%

profile of v3, /device:TPU:8, one launch (start us, length us, event | category | flops | bytes accessed | tf_op | source)
XLA Modules:
  0.0 140.0 jit_solution(14979026538222905577)
XLA Ops:
  7.2 0.0 copy-start.2
  7.2 0.0 all-gather.2.cloned.1.call-start
  7.2 2.5 %shard_map.67 = f32[16,32,128]{2,1,0:T(8,128)} custom-call(f32[64,448]{1,0:T(8,128)} %bitcast.27, bf16[448,1024]{1,0:T(8,128)(2,1)} %bitcast.30), custom_call_target="tpu_custom_call" | custom-call | tf_op jit(solution)/shard_map/pallas_call | solution.py:48
  9.7 0.0 all-gather.2.cloned.1.call-update
  9.7 10.4 %all-to-all-start = ((f32[16,32,128]{2,1,0:T(8,128)}), f32[16,32,128]{2,1,0:T(8,128)S(1)}, u32[]{:S(2)}, u32[]{:S(2)}) async-start(f32[16,32,128]{2,1,0:T(8,128)} %shard_map.67), calls=%async_computation | async-start | bytes 524288 | tf_op jit(solution)/shard_map/all_to_all | solution.py:294
  20.1 0.0 copy-start
  20.2 1.5 %copy-done = bf16[1,2048,448]{1,2,0:T(8,128)(2,1)S(1)} copy-done((bf16[1,2048,448]{1,2,0:T(8,128)(2,1)S(1)}, bf16[1,2048,448]{1,2,0:T(8,128)(2,1)}, u32[]{:S(2)}) %copy-start) | copy-done | bytes 1835032
  21.7 0.0 copy-start.4
  21.7 0.9 copy-done.4
  22.6 0.6 shard_map.68.pf_ref
  23.1 8.2 %all-to-all-done.y_ref = f32[16,32,128]{2,1,0:T(8,128)S(1)} async-done(((f32[16,32,128]{2,1,0:T(8,128)}), f32[16,32,128]{2,1,0:T(8,128)S(1)}, u32[]{:S(2)}, u32[]{:S(2)}) %all-to-all-start) | async-done | bytes 262176 | tf_op jit(solution)/shard_map/all_to_all | solution.py:294
  31.3 0.0 copy-done.2
  31.3 0.4 shard_map.69
  31.8 4.7 %all_to_all.35.x_ref = f32[2,512,128]{2,1,0:T(8,128)S(1)} all-to-all(f32[2,512,128]{2,1,0:T(8,128)S(1)} %bitcast.23), channel_id=1, replica_groups=mesh['x'=4,'y'=8,'z'=8,'c'=2] {'c'}, dimensions={0} | all-to-all | bytes 1048576 | tf_op jit(solution)/shard_map/all_to_all | solution.py:300
  36.5 22.5 %all_to_all.36.refs_0_ = f32[32,16,128]{2,1,0:T(8,128)S(1)} all-to-all(f32[32,16,128]{2,1,0:T(8,128)S(1)} %bitcast.24), channel_id=1, replica_groups=mesh['x'=4,'y'=8,'z'=8,'c'=2] {'x','y'}, dimensions={0} | all-to-all | bytes 524288 | tf_op jit(solution)/shard_map/all_to_all | solution.py:302
  59.0 11.1 %all_to_all.37.refs_0_ = f32[8,16,128]{2,1,0:T(8,128)S(1)} all-to-all(f32[8,16,128]{2,1,0:T(8,128)S(1)} %shard_map.71), channel_id=1, replica_groups=mesh['x'=4,'y'=8,'z'=8,'c'=2] {'z'}, dimensions={0} | all-to-all | bytes 131072 | tf_op jit(solution)/shard_map/all_to_all | solution.py:304
  70.1 0.7 shard_map.72
  70.8 4.6 %all-to-all-start.4 = ((f32[32,16,128]{2,1,0:T(8,128)}), f32[32,16,128]{2,1,0:T(8,128)S(1)}, u32[]{:S(2)}, u32[]{:S(2)}) async-start(f32[32,16,128]{2,1,0:T(8,128)} %shard_map.72), calls=%async_computation.4 | async-start | bytes 524288 | tf_op jit(solution)/shard_map/all_to_all | solution.py:306
  75.4 0.0 all-gather.2.cloned.1.call-done.a_ref.a_hbm
  75.4 7.3 %shard_map.73.c_ref = f32[448,2048]{1,0:T(8,128)} custom-call(bf16[1024,2048]{1,0:T(8,128)(2,1)} %all-gather.2.cloned.1.call-done.a_ref.a_hbm, bf16[448,1024]{1,0:T(8,128)(2,1)} %bitcast.31, bf16[448,2048]{1,0:T(8,128)(2,1)} %bitcast.20), custom_call_target="tpu_custom_call" | custom-call | flops 1879048192 | bytes 12582912 | tf_op jit(solution)/shard_map/pallas_call | solution.py:48
  82.7 3.7 %all-to-all-done.4 = f32[32,16,128]{2,1,0:T(8,128)S(1)} async-done(((f32[32,16,128]{2,1,0:T(8,128)}), f32[32,16,128]{2,1,0:T(8,128)S(1)}, u32[]{:S(2)}, u32[]{:S(2)}) %all-to-all-start.4) | async-done | bytes 262176 | tf_op jit(solution)/shard_map/all_to_all | solution.py:306
  86.5 0.0 copy-start.5
  86.5 1.9 %collective-permute-start = (f32[8,64,128]{2,1,0:T(8,128)S(1)}, f32[8,64,128]{2,1,0:T(8,128)S(1)}, u32[]{:S(2)}, u32[]{:S(2)}) collective-permute-start(f32[8,64,128]{2,1,0:T(8,128)S(1)} %bitcast.33), channel_id=1, source_target_pairs={{0,1},{1,0},{2,3},{3,2},{4,5},{5,4},{6,7},{7,6},{8,9},{9,8},{10,11... | collective-permute-start | bytes 786440 | tf_op jit(solution)/shard_map/ppermute | solution.py:330
  88.4 0.6 pad_add_fusion.place_ref
  89.0 0.0 copy-start.1
  89.0 0.9 collective-permute-done.other_ref
  89.9 0.0 copy-done.5
  89.9 0.0 copy-start.6
  89.9 0.7 copy-done.6
  90.6 9.0 %shard_map.74 = (f32[16,64,128]{2,1,0:T(8,128)}, f32[64,128]{1,0:T(8,128)}, f32[4,64,128]{2,1,0:T(8,128)}) custom-call(s32[2]{0:T(128)} %pad_add_fusion.place_ref, f32[8,64,128]{2,1,0:T(8,128)} %bitcast.34, f32[8,64,128]{2,1,0:T(8,128)} %copy-done.6, bf16[1024,2048]{1,0:T(8,128)(2,1)} %all-gather.2.cloned.1.call-done.a_ref.a_hbm, ...), custom_call_target="tpu_custom_call" | custom-call | tf_op jit(solution)/shard_map/pallas_call | solution.py:48
  99.6 16.1 %all_to_all.38.refs_0_ = f32[32,8,128]{2,1,0:T(8,128)S(1)} all-to-all(f32[32,8,128]{2,1,0:T(8,128)} %bitcast.35), channel_id=1, replica_groups=mesh['x'=4,'y'=8,'z'=8,'c'=2] {'x','y'}, dimensions={0} | all-to-all | bytes 262144 | tf_op jit(solution)/shard_map/all_to_all | solution.py:354
  115.7 13.9 %all_to_all.39 = f32[32,8,128]{2,1,0:T(8,128)S(1)} all-to-all(f32[32,8,128]{2,1,0:T(8,128)S(1)} %shard_map.75), channel_id=1, replica_groups=mesh['x'=4,'y'=8,'z'=8,'c'=2] {'x','y'}, dimensions={0} | all-to-all | bytes 262144 | tf_op jit(solution)/shard_map/all_to_all | solution.py:356
  129.6 0.0 copy-done.1
  129.6 0.0 copy-start.3
  129.6 1.0 copy-done.3
  130.7 2.5 %shard_map.76 = (bf16[448,2048]{1,0:T(8,128)(2,1)}, f32[64,448]{1,0:T(8,128)}) custom-call(f32[4,64,128]{2,1,0:T(8,128)S(1)} %bitcast.29, f32[16,64,128]{2,1,0:T(8,128)S(1)} %copy-done.3, f32[448,2048]{1,0:T(8,128)S(1)} %copy-done.1), custom_call_target="tpu_custom_call" | custom-call | tf_op jit(solution)/shard_map/pallas_call | solution.py:48
  (3 shorter events, 0.1 us)
Async XLA Ops:
  7.2 24.2 %copy-start.2 = (bf16[1,64,2048]{2,1,0:T(8,128)(2,1)S(1)}, bf16[1,64,2048]{2,1,0:T(8,128)(2,1)}, u32[]{:S(2)}) copy-start(bf16[1,64,2048]{2,1,0:T(8,128)(2,1)} %param.4) | copy-start | bytes 786436
  7.2 68.3 %all-gather.2.cloned.1.call-start = ((), (), s32[]{:S(2)}) async-start(), calls=%async_computation.7 | async-start | bytes 4456448 | tf_op jit(solution)/shard_map/all_gather | solution.py:293
  9.7 21.6 %all-to-all-start = ((f32[16,32,128]{2,1,0:T(8,128)}), f32[16,32,128]{2,1,0:T(8,128)S(1)}, u32[]{:S(2)}, u32[]{:S(2)}) async-start(f32[16,32,128]{2,1,0:T(8,128)} %shard_map.67), calls=%async_computation | async-start | bytes 524288 | tf_op jit(solution)/shard_map/all_to_all | solution.py:294
  20.1 1.5 %copy-start = (bf16[1,2048,448]{1,2,0:T(8,128)(2,1)S(1)}, bf16[1,2048,448]{1,2,0:T(8,128)(2,1)}, u32[]{:S(2)}) copy-start(bf16[1,2048,448]{1,2,0:T(8,128)(2,1)} %param.6) | copy-start | bytes 5505028
  21.7 0.9 copy-start.4
  70.8 15.6 %all-to-all-start.4 = ((f32[32,16,128]{2,1,0:T(8,128)}), f32[32,16,128]{2,1,0:T(8,128)S(1)}, u32[]{:S(2)}, u32[]{:S(2)}) async-start(f32[32,16,128]{2,1,0:T(8,128)} %shard_map.72), calls=%async_computation.4 | async-start | bytes 524288 | tf_op jit(solution)/shard_map/all_to_all | solution.py:306
  86.5 3.4 %copy-start.5 = (f32[32,16,128]{2,1,0:T(8,128)}, f32[32,16,128]{2,1,0:T(8,128)S(1)}, u32[]{:S(2)}) copy-start(f32[32,16,128]{2,1,0:T(8,128)S(1)} %all-to-all-done.4) | copy-start | bytes 786436
  86.5 3.4 %collective-permute-start = (f32[8,64,128]{2,1,0:T(8,128)S(1)}, f32[8,64,128]{2,1,0:T(8,128)S(1)}, u32[]{:S(2)}, u32[]{:S(2)}) collective-permute-start(f32[8,64,128]{2,1,0:T(8,128)S(1)} %bitcast.33), channel_id=1, source_target_pairs={{0,1},{1,0},{2,3},{3,2},{4,5},{5,4},{6,7},{7,6},{8,9},{9,8},{10,11... | collective-permute-start | bytes 786440 | tf_op jit(solution)/shard_map/ppermute | solution.py:330
  89.0 40.6 %copy-start.1 = (f32[448,2048]{1,0:T(8,128)S(1)}, f32[448,2048]{1,0:T(8,128)}, u32[]{:S(2)}) copy-start(f32[448,2048]{1,0:T(8,128)} %shard_map.73.c_ref) | copy-start | bytes 11010052
  89.9 0.7 copy-start.6
  129.6 1.0 copy-start.3
Sparse Core Ops, SparseCore 0:
  10.1 49.7 all-gather.1

commit v4 on v3

--- a/solution.py
+++ b/solution.py
@@ -211,14 +211,14 @@
 
 
 def factors_kernel(
-    place_ref, mine_ref, other_ref, a_hbm, f_hbm, g_hbm,
+    place_ref, mine_ref, other_ref, high_hbm, middle_hbm,
     p_ref, p_mine_ref, out_ref,
-    kept_ref, a_ref, f_ref, g_ref, sems,
+    kept_ref, high_ref, middle_ref, sems,
 ):
     tiles = p_ref.shape[0]
     part = tiles // 2
     member, core = place_ref[0], place_ref[1]
-    copies = started((a_hbm, f_hbm, g_hbm), (a_ref, f_ref, g_ref), sems)
+    copies = started((high_hbm, middle_hbm), (high_ref, middle_ref), sems)
     for ref in (p_ref, kept_ref):
         ref[pl.ds(core * part, part)] = mine_ref[...]
         ref[pl.ds((1 - core) * part, part)] = other_ref[...]
@@ -227,8 +227,10 @@
     p = wide(p_ref)
     for copy in copies:
         copy.wait()
-    product = pair_dot_t(p, f_ref[...])
-    product = product + pair_dot_t(pair_dot_t(p, a_ref[...]), g_ref[...])
+    product = pair_dot_t(p, high_ref[...])
+    product = product + lax.dot_general(
+        p.astype(BF16), middle_ref[...], (((1,), (1,)), ((), ())), preferred_element_type=F32
+    )
     width = product.shape[1]
     for tile in range(out_ref.shape[0]):
         block = product[:, tile * LANES : min(width, (tile + 1) * LANES)]
@@ -237,9 +239,27 @@
         out_ref[tile] = block
 
 
-def corrected_kernel(a_ref, g_ref, f_ref, out_ref):
-    product = jnp.dot(g_ref[...], a_ref[...], preferred_element_type=F32)
-    out_ref[...] = product + f_ref[...].astype(F32)
+def corrected_kernel(
+    a_hbm, g_hbm, f_hbm, out_hbm, high_hbm, middle_hbm,
+    a_ref, g_ref, f_ref, out_ref, high_ref, middle_ref, sems, out_sems,
+):
+    steps = out_sems.shape[1]
+    step = out_ref.shape[1] // steps
+    for copy in started((g_hbm, a_hbm, f_hbm), (g_ref, a_ref, f_ref), sems):
+        copy.wait()
+    writes = []
+    for i in range(steps):
+        at = pl.ds(i * step, step)
+        product = jnp.dot(g_ref[...], a_ref[:, at], preferred_element_type=F32)
+        corrected = product + f_ref[:, at].astype(F32)
+        out_ref[:, at] = corrected
+        high_ref[:, at], middle_ref[:, at], _ = split3(corrected)
+        refs = ((out_ref, out_hbm), (high_ref, high_hbm), (middle_ref, middle_hbm))
+        for j, (source, target) in enumerate(refs):
+            writes.append(pltpu.make_async_copy(source.at[:, at], target.at[:, at], out_sems.at[j, i]))
+            writes[-1].start()
+    for write in writes:
+        write.wait()
 
 
 def feedback_out_kernel(q_ref, p_ref, c_ref, fb_hbm, qt_ref, fb_ref, fb_sems):
@@ -305,27 +325,31 @@
     p = share(p, replicas, 1.0)
     p = lax.all_to_all(p, xy, 0, 0).reshape(tiles // 2, rank, LANES)
 
-    rows = columns // 4
-    block = pl.BlockSpec((rows, width), lambda i: (i, 0))
-    corrected = call(
+    steps = 4
+    corrected, high, middle = call(
         corrected_kernel,
-        ((columns, width), F32),
+        [((columns, width), F32), ((columns, width), BF16), ((columns, width), BF16)],
         a_full,
         gt,
         ft,
-        grid=(columns // rows,),
-        in_specs=[
-            pl.BlockSpec((tokens, width), lambda i: (0, 0)),
-            pl.BlockSpec((rows, tokens), lambda i: (i, 0)),
-            block,
+        in_specs=[hbm] * 3,
+        out_specs=[hbm] * 3,
+        scratch_shapes=[
+            pltpu.VMEM(a_full.shape, BF16),
+            pltpu.VMEM(gt.shape, BF16),
+            pltpu.VMEM(ft.shape, BF16),
+            pltpu.VMEM((columns, width), F32),
+            pltpu.VMEM((columns, width), BF16),
+            pltpu.VMEM((columns, width), BF16),
+            pltpu.SemaphoreType.DMA((3,)),
+            pltpu.SemaphoreType.DMA((3, steps)),
         ],
-        out_specs=block,
         vmem=57,
         cost_estimate=pl.CostEstimate(
             flops=2 * columns * width * tokens, bytes_accessed=12 * 2**20, transcendentals=0
         ),
     )
-    p, corrected = lax.optimization_barrier((p, corrected))
+    p, corrected, high, middle = lax.optimization_barrier((p, corrected, high, middle))
 
     p_other = lax.ppermute(p, "c", swap)
     q_tiles = -(-columns // LANES)
@@ -336,19 +360,17 @@
         place,
         p,
         p_other,
-        a_full,
-        ft,
-        gt,
-        in_specs=[smem, vmem, vmem] + [hbm] * 3,
+        high,
+        middle,
+        in_specs=[smem, vmem, vmem, hbm, hbm],
         out_specs=[vmem] * 3,
         scratch_shapes=[
             pltpu.VMEM((tiles, rank, LANES), F32),
-            pltpu.VMEM(a_full.shape, BF16),
-            pltpu.VMEM(ft.shape, BF16),
-            pltpu.VMEM(gt.shape, BF16),
-            pltpu.SemaphoreType.DMA((3,)),
+            pltpu.VMEM(high.shape, BF16),
+            pltpu.VMEM(middle.shape, BF16),
+            pltpu.SemaphoreType.DMA((2,)),
         ],
-        vmem=54,
+        vmem=57,
     )
 
     q = lax.all_to_all(q.reshape(replicas, -1, LANES), xy, 0, 0)

time: 141 us -> 139 us (0.986)
  waiting for transfers between devices: 12.9 us -> 15.6 us
  local copies, waits for them, and re-layouts: 4.19 us -> 1.79 us
    unnamed x14, local copies, waits for them, and re-layouts: 4.19 us -> 1.79 us
    all_to_all x1, waiting for transfers between devices: 8.19 us -> 10.6 us  [body(): y = lax.all_to_all(y, tensor, 0, 0)]
    pallas_call x10, Pallas kernels: 23 us -> 21.6 us  [call(): pl.pallas_call(kernel, out_shape=shapes, compiler_params=pltpu.CompilerPa...]
where the time goes in v4:
time: 139 us
  blocking collectives  67.8 us (49%)
  Pallas kernels  21.6 us (16%)
  starting transfers between devices  17.1 us (12%)
  waiting for transfers between devices  15.6 us (11%)
  between operations  14.2 us (10%)
  local copies, waits for them, and re-layouts  1.79 us (1%)
    all_to_all x1, blocking collectives, body(): p = lax.all_to_all(p.reshape(replicas, -1, LANES), xy, 0, 0)  22.6 us
    pallas_call x10, Pallas kernels, call(): pl.pallas_call(kernel, out_shape=shapes, compiler_params=pltpu.CompilerPa...  21.6 us
    all_to_all x1, blocking collectives, body(): q = lax.all_to_all(q.reshape(replicas, -1, LANES), xy, 0, 0)  15.7 us
    all_to_all x1, blocking collectives, body(): q = lax.all_to_all(q, xy, 0, 0).reshape(q_tiles, rank, LANES)  13.9 us
    all_to_all x1, blocking collectives, body(): p = lax.all_to_all(p, 'z', 0, 0)  11 us
    all_to_all x1, waiting for transfers between devices, body(): y = lax.all_to_all(y, tensor, 0, 0)  10.6 us
    all_to_all x1, starting transfers between devices, body(): y = lax.all_to_all(y, tensor, 0, 0)  10.6 us
    all_to_all x1, blocking collectives, body(): p = lax.all_to_all(p.reshape(2, tiles // 2 * rank, LANES), 'c', 0, 0)  4.59 us
  transfers between devices with their start and end apart: 4, of which 3 were waited for; matrix products, arithmetic and copies ran while one was open for 0% of the time, Pallas kernels for 6%

profile of v4, /device:TPU:8, one launch (start us, length us, event | category | flops | bytes accessed | tf_op | source)
XLA Modules:
  0.0 138.7 jit_solution(14998511935416653731)
XLA Ops:
  7.2 0.0 copy-start.4
  7.2 0.0 copy-start.1
  7.2 0.0 all-gather.2.cloned.1.call-start
  7.2 2.5 %shard_map.67 = f32[16,32,128]{2,1,0:T(8,128)} custom-call(f32[64,448]{1,0:T(8,128)} %bitcast.26, bf16[448,1024]{1,0:T(8,128)(2,1)} %bitcast.31), custom_call_target="tpu_custom_call" | custom-call | tf_op jit(solution)/shard_map/pallas_call | solution.py:48
  9.8 0.0 copy-start.2
  9.8 0.0 all-gather.2.cloned.1.call-update
  9.8 10.6 %all-to-all-start = ((f32[16,32,128]{2,1,0:T(8,128)}), f32[16,32,128]{2,1,0:T(8,128)S(1)}, u32[]{:S(2)}, u32[]{:S(2)}) async-start(f32[16,32,128]{2,1,0:T(8,128)} %shard_map.67), calls=%async_computation | async-start | bytes 524288 | tf_op jit(solution)/shard_map/all_to_all | solution.py:314
  20.4 0.0 copy-done.4
  20.4 0.0 copy-done.1
  20.4 0.6 shard_map.68.pf_ref
  21.0 10.6 %all-to-all-done.y_ref = f32[16,32,128]{2,1,0:T(8,128)S(1)} async-done(((f32[16,32,128]{2,1,0:T(8,128)}), f32[16,32,128]{2,1,0:T(8,128)S(1)}, u32[]{:S(2)}, u32[]{:S(2)}) %all-to-all-start) | async-done | bytes 262176 | tf_op jit(solution)/shard_map/all_to_all | solution.py:314
  31.6 0.0 copy-done.2
  31.6 0.4 shard_map.69
  32.0 4.6 %all_to_all.35.x_ref = f32[2,512,128]{2,1,0:T(8,128)S(1)} all-to-all(f32[2,512,128]{2,1,0:T(8,128)S(1)} %bitcast.20), channel_id=1, replica_groups=mesh['x'=4,'y'=8,'z'=8,'c'=2] {'c'}, dimensions={0} | all-to-all | bytes 1048576 | tf_op jit(solution)/shard_map/all_to_all | solution.py:320
  36.6 22.6 %all_to_all.36.refs_0_ = f32[32,16,128]{2,1,0:T(8,128)S(1)} all-to-all(f32[32,16,128]{2,1,0:T(8,128)S(1)} %bitcast.23), channel_id=1, replica_groups=mesh['x'=4,'y'=8,'z'=8,'c'=2] {'x','y'}, dimensions={0} | all-to-all | bytes 524288 | tf_op jit(solution)/shard_map/all_to_all | solution.py:322
  59.3 11.0 %all_to_all.37.refs_0_ = f32[8,16,128]{2,1,0:T(8,128)S(1)} all-to-all(f32[8,16,128]{2,1,0:T(8,128)S(1)} %shard_map.71), channel_id=1, replica_groups=mesh['x'=4,'y'=8,'z'=8,'c'=2] {'z'}, dimensions={0} | all-to-all | bytes 131072 | tf_op jit(solution)/shard_map/all_to_all | solution.py:324
  70.3 0.7 shard_map.72
  71.1 4.6 %all-to-all-start.4 = ((f32[32,16,128]{2,1,0:T(8,128)}), f32[32,16,128]{2,1,0:T(8,128)S(1)}, u32[]{:S(2)}, u32[]{:S(2)}) async-start(f32[32,16,128]{2,1,0:T(8,128)} %shard_map.72), calls=%async_computation.4 | async-start | bytes 524288 | tf_op jit(solution)/shard_map/all_to_all | solution.py:326
  75.6 0.0 all-gather.2.cloned.1.call-done.a_hbm
  75.7 6.9 %shard_map.73 = (f32[448,2048]{1,0:T(8,128)}, bf16[448,2048]{1,0:T(8,128)(2,1)}, bf16[448,2048]{1,0:T(8,128)(2,1)}) custom-call(bf16[1024,2048]{1,0:T(8,128)(2,1)} %all-gather.2.cloned.1.call-done.a_hbm, bf16[448,1024]{1,0:T(8,128)(2,1)} %bitcast.32, bf16[448,2048]{1,0:T(8,128)(2,1)} %bitcast.21), custom_call_target="tpu_custom_call" | custom-call | flops 1879048192 | bytes 12582912 | tf_op jit(solution)/shard_map/pallas_call | solution.py:48
  82.6 4.1 %all-to-all-done.4 = f32[32,16,128]{2,1,0:T(8,128)S(1)} async-done(((f32[32,16,128]{2,1,0:T(8,128)}), f32[32,16,128]{2,1,0:T(8,128)S(1)}, u32[]{:S(2)}, u32[]{:S(2)}) %all-to-all-start.4) | async-done | bytes 262176 | tf_op jit(solution)/shard_map/all_to_all | solution.py:326
  86.7 0.0 copy-start.5
  86.7 1.9 %collective-permute-start = (f32[8,64,128]{2,1,0:T(8,128)S(1)}, f32[8,64,128]{2,1,0:T(8,128)S(1)}, u32[]{:S(2)}, u32[]{:S(2)}) collective-permute-start(f32[8,64,128]{2,1,0:T(8,128)S(1)} %bitcast.29), channel_id=1, source_target_pairs={{0,1},{1,0},{2,3},{3,2},{4,5},{5,4},{6,7},{7,6},{8,9},{9,8},{10,11... | collective-permute-start | bytes 786440 | tf_op jit(solution)/shard_map/ppermute | solution.py:354
  88.6 0.7 pad_add_fusion.place_ref
  89.3 0.0 copy-start
  89.3 0.8 collective-permute-done.other_ref
  90.1 0.0 copy-done.5
  90.1 0.0 copy-start.6
  90.1 0.7 copy-done.6
  90.8 7.8 %shard_map.74 = (f32[16,64,128]{2,1,0:T(8,128)}, f32[64,128]{1,0:T(8,128)}, f32[4,64,128]{2,1,0:T(8,128)}) custom-call(s32[2]{0:T(128)} %pad_add_fusion.place_ref, f32[8,64,128]{2,1,0:T(8,128)} %bitcast.30, f32[8,64,128]{2,1,0:T(8,128)} %copy-done.6, bf16[448,2048]{1,0:T(8,128)(2,1)} %get-tuple-element.23.high_hbm, ...), custom_call_target="tpu_custom_call" | custom-call | tf_op jit(solution)/shard_map/pallas_call | solution.py:48
  98.7 15.7 %all_to_all.38.refs_0_ = f32[32,8,128]{2,1,0:T(8,128)S(1)} all-to-all(f32[32,8,128]{2,1,0:T(8,128)} %bitcast.33), channel_id=1, replica_groups=mesh['x'=4,'y'=8,'z'=8,'c'=2] {'x','y'}, dimensions={0} | all-to-all | bytes 262144 | tf_op jit(solution)/shard_map/all_to_all | solution.py:376
  114.4 13.9 %all_to_all.39 = f32[32,8,128]{2,1,0:T(8,128)S(1)} all-to-all(f32[32,8,128]{2,1,0:T(8,128)S(1)} %shard_map.75), channel_id=1, replica_groups=mesh['x'=4,'y'=8,'z'=8,'c'=2] {'x','y'}, dimensions={0} | all-to-all | bytes 262144 | tf_op jit(solution)/shard_map/all_to_all | solution.py:378
  128.3 0.0 copy-done
  128.3 0.0 copy-start.3
  128.3 1.0 copy-done.3
  129.4 2.5 %shard_map.76 = (bf16[448,2048]{1,0:T(8,128)(2,1)}, f32[64,448]{1,0:T(8,128)}) custom-call(f32[4,64,128]{2,1,0:T(8,128)S(1)} %bitcast.28, f32[16,64,128]{2,1,0:T(8,128)S(1)} %copy-done.3, f32[448,2048]{1,0:T(8,128)S(1)} %copy-done), custom_call_target="tpu_custom_call" | custom-call | tf_op jit(solution)/shard_map/pallas_call | solution.py:48
  (3 shorter events, 0.1 us)
Async XLA Ops:
  7.2 13.2 %copy-start.4 = (f32[448,64]{0,1:T(8,128)S(1)}, f32[448,64]{0,1:T(8,128)}, u32[]{:S(2)}) copy-start(f32[448,64]{0,1:T(8,128)} %param.7) | copy-start | bytes 344068
  7.2 13.2 %copy-start.1 = (bf16[1,2048,448]{1,2,0:T(8,128)(2,1)S(1)}, bf16[1,2048,448]{1,2,0:T(8,128)(2,1)}, u32[]{:S(2)}) copy-start(bf16[1,2048,448]{1,2,0:T(8,128)(2,1)} %param.6) | copy-start | bytes 5505028
  7.2 68.5 %all-gather.2.cloned.1.call-start = ((), (), s32[]{:S(2)}) async-start(), calls=%async_computation.7 | async-start | bytes 4456448 | tf_op jit(solution)/shard_map/all_gather | solution.py:313
  9.8 21.8 %copy-start.2 = (bf16[1,64,2048]{2,1,0:T(8,128)(2,1)S(1)}, bf16[1,64,2048]{2,1,0:T(8,128)(2,1)}, u32[]{:S(2)}) copy-start(bf16[1,64,2048]{2,1,0:T(8,128)(2,1)} %param.4) | copy-start | bytes 786436
  9.8 21.7 %all-to-all-start = ((f32[16,32,128]{2,1,0:T(8,128)}), f32[16,32,128]{2,1,0:T(8,128)S(1)}, u32[]{:S(2)}, u32[]{:S(2)}) async-start(f32[16,32,128]{2,1,0:T(8,128)} %shard_map.67), calls=%async_computation | async-start | bytes 524288 | tf_op jit(solution)/shard_map/all_to_all | solution.py:314
  71.1 15.6 %all-to-all-start.4 = ((f32[32,16,128]{2,1,0:T(8,128)}), f32[32,16,128]{2,1,0:T(8,128)S(1)}, u32[]{:S(2)}, u32[]{:S(2)}) async-start(f32[32,16,128]{2,1,0:T(8,128)} %shard_map.72), calls=%async_computation.4 | async-start | bytes 524288 | tf_op jit(solution)/shard_map/all_to_all | solution.py:326
  86.7 3.4 %copy-start.5 = (f32[32,16,128]{2,1,0:T(8,128)}, f32[32,16,128]{2,1,0:T(8,128)S(1)}, u32[]{:S(2)}) copy-start(f32[32,16,128]{2,1,0:T(8,128)S(1)} %all-to-all-done.4) | copy-start | bytes 786436
  86.7 3.4 %collective-permute-start = (f32[8,64,128]{2,1,0:T(8,128)S(1)}, f32[8,64,128]{2,1,0:T(8,128)S(1)}, u32[]{:S(2)}, u32[]{:S(2)}) collective-permute-start(f32[8,64,128]{2,1,0:T(8,128)S(1)} %bitcast.29), channel_id=1, source_target_pairs={{0,1},{1,0},{2,3},{3,2},{4,5},{5,4},{6,7},{7,6},{8,9},{9,8},{10,11... | collective-permute-start | bytes 786440 | tf_op jit(solution)/shard_map/ppermute | solution.py:354
  89.3 39.0 %copy-start = (f32[448,2048]{1,0:T(8,128)S(1)}, f32[448,2048]{1,0:T(8,128)}, u32[]{:S(2)}) copy-start(f32[448,2048]{1,0:T(8,128)} %get-tuple-element.27.c_ref) | copy-start | bytes 11010052
  90.1 0.7 copy-start.6
  128.3 1.0 copy-start.3
Sparse Core Ops, SparseCore 0:
  10.1 50.2 all-gather.1
